TPU v7x, 32 devices: a whole 2x2x4 slice. The times are simulated.
32 devices in a mesh: rep: 4 (over x, core), gx: 2 (over y), gy: 4 (over z).
Axes of the slice: x: 2, y: 2, z: 4, core: 2. Of those that a mesh axis runs over, the one named last changes fastest.
Arguments:
- node_feat: bfloat16 [8192, 256], P(('rep', 'gx', 'gy')), may hold values from -6 to 6
- edge_feat: bfloat16 [262144, 256], P(('rep', 'gx', 'gy')), may hold values from -6 to 6
- edge_src: int32 [262144], P(('rep', 'gx', 'gy')), may hold values from 0 to 1023
- edge_dst: int32 [262144], P(('rep', 'gx', 'gy')), may hold values from 0 to 255
- edge_count: int32 [32], P(('rep', 'gx', 'gy')), may hold values from 2048 to 8192, as said below
- send_idx: int32 [4, 2, 4, 2, 2, 64], P('rep', 'gx', 'gy'), may hold values from 0 to 255
- w_qkv: bfloat16 [2, 256, 768], replicated, may hold values from -0.375 to 0.375
- w_edge: bfloat16 [2, 256, 256], replicated, may hold values from -0.375 to 0.375
- gains: float32 [2, 256], replicated, may hold values from 0.1 to 1.9
- head_in: bfloat16 [256, 256], replicated, may hold values from -0.375 to 0.375
- head_out: bfloat16 [256, 169], replicated, may hold values from -0.375 to 0.375
- targets: bfloat16 [169, 262144], P(None, ('rep', 'gx', 'gy')), may hold values from -15 to 15
Outputs:
- node_out: bfloat16 [8192, 256], P(('rep', 'gx', 'gy'))
- grad_head_in: float32 [256, 256], replicated
- grad_head_out: float32 [256, 169], replicated
Inputs may be any that keep to these rules, and one draw needn't show every extreme that they name: `edge_count`: edge slots of a tile at positions from its count on are padding; some tile holds 8192 live edges.
All inputs are finite; a program needn't handle non-finite values.
Results may differ from a plain program's by a relative error of at most 0.0025.
The roundings to bfloat16 on the way count: a program that leaves them out, or rounds other values in their place, can miss the bound.
Values may be sent and summed in bfloat16 or wider, within the bound.
A program may use at most 128 MiB of HBM per device.

v0:
```python
import math

import jax
import jax.numpy as jnp
from jax import lax
from jax.sharding import PartitionSpec as P

OUTER_CELLS = (
    (0, 0),
    (0, 1),
    (0, 2),
    (0, 3),
    (1, 0),
    (1, 3),
    (2, 0),
    (2, 3),
    (3, 0),
    (3, 1),
    (3, 2),
    (3, 3),
)


def with_halo(x, sides, width):
    for axis, dim in sides:
        count, length = (lax.axis_size(axis), x.shape[dim])
        up = [(i, (i + 1) % count) for i in range(count)]
        down = [(j, i) for i, j in up]
        last = lax.slice_in_dim(x, length - width, length, axis=dim)
        initial = lax.slice_in_dim(x, 0, width, axis=dim)
        before = lax.ppermute(last, axis, up)
        after = lax.ppermute(initial, axis, down)
        x = jnp.concatenate([before, x, after], axis=dim)
    return x


def layer_norm(values):
    centre = values - jnp.mean(values, axis=-1, keepdims=True)
    spread = jnp.mean(centre * centre, axis=-1, keepdims=True)
    return centre * lax.rsqrt(spread + 1e-05)


def outer_rows(padded):
    return jnp.concatenate([padded[cell_i, cell_j] for cell_i, cell_j in OUTER_CELLS], axis=0)


def edge_pass(table, query_part, edges, edge_src, edge_dst, live_column, weight_edge):
    edge_slots, feature_width = edges.shape
    atom_count = query_part.shape[0]
    table_rows = table.shape[0]
    block_rows = math.gcd(edge_slots, 2048)
    block_count = edge_slots // block_rows
    table_iota = jnp.arange(table_rows, dtype=jnp.int32)
    atom_iota = jnp.arange(atom_count, dtype=jnp.int32)

    def one_block(carry, items):
        edge_rows, source_rows, target_rows, live_rows = items
        source_hot = (source_rows[:, None] == table_iota[None, :]).astype(jnp.bfloat16)
        target_hot = (target_rows[:, None] == atom_iota[None, :]).astype(jnp.bfloat16)
        gathered = jnp.dot(source_hot, table, preferred_element_type=jnp.float32)
        queries = jnp.dot(target_hot, query_part, preferred_element_type=jnp.float32)
        pre_act = queries + gathered[:, :feature_width]
        pre_act = pre_act + jnp.dot(edge_rows, weight_edge, preferred_element_type=jnp.float32)
        new_rows = (edge_rows.astype(jnp.float32) + live_rows * jax.nn.silu(pre_act)).astype(
            jnp.bfloat16
        )
        weighted = live_rows * jax.nn.sigmoid(pre_act) * gathered[:, feature_width:]
        added = lax.dot_general(
            target_hot.astype(jnp.float32),
            weighted,
            (((0,), (0,)), ((), ())),
            precision=lax.Precision.HIGHEST,
            preferred_element_type=jnp.float32,
        )
        return (carry + added, new_rows)

    start = jnp.zeros((atom_count, feature_width), jnp.float32)
    items = (
        edges.reshape(block_count, block_rows, feature_width),
        edge_src.reshape(block_count, block_rows),
        edge_dst.reshape(block_count, block_rows),
        live_column.reshape(block_count, block_rows, 1),
    )
    summed, new_blocks = lax.scan(one_block, start, items)
    return (summed, new_blocks.reshape(edge_slots, feature_width))


def body(
    node_feat,
    edge_feat,
    edge_src,
    edge_dst,
    edge_count,
    send_idx,
    w_qkv,
    w_edge,
    gains,
    head_in,
    head_out,
    targets,
):
    feature_width = node_feat.shape[1]
    edge_slots = edge_feat.shape[0]
    cell_rows = send_idx.shape[-1]
    corner_index = send_idx.reshape(2, 2, cell_rows)
    positions = jnp.arange(edge_slots, dtype=jnp.int32)
    live_column = (positions < edge_count[0]).astype(jnp.float32)[:, None]
    nodes = node_feat
    edges = edge_feat
    for layer_index in range(w_qkv.shape[0]):
        weight_qkv = w_qkv[layer_index]
        projected = jnp.dot(nodes, weight_qkv, preferred_element_type=jnp.float32).astype(
            jnp.bfloat16
        )
        local_kv = projected[:, feature_width:]
        padded = with_halo(nodes[corner_index], (("gx", 0), ("gy", 1)), 1)
        ghost_kv = jnp.dot(
            outer_rows(padded), weight_qkv[:, feature_width:], preferred_element_type=jnp.float32
        ).astype(jnp.bfloat16)
        table = jnp.concatenate([local_kv, ghost_kv], axis=0)
        summed, edges = edge_pass(
            table,
            projected[:, :feature_width],
            edges,
            edge_src,
            edge_dst,
            live_column,
            w_edge[layer_index],
        )
        nodes = (nodes.astype(jnp.float32) + gains[layer_index] * layer_norm(summed)).astype(
            jnp.bfloat16
        )
    scale = 0.125 / (edge_slots * lax.axis_size(("rep", "gx", "gy"))) ** 0.5
    act_in = jnp.dot(edges, head_in, preferred_element_type=jnp.float32)
    hidden_head = jax.nn.silu(act_in).astype(jnp.bfloat16)
    pred = lax.dot_general(
        head_out, hidden_head, (((0,), (1,)), ((), ())), preferred_element_type=jnp.float32
    )
    live_row = live_column[:, 0][None, :]
    dpred = (live_row * (pred - targets.astype(jnp.float32)) * scale).astype(jnp.bfloat16)
    dhidden = lax.dot_general(
        dpred, head_out, (((0,), (1,)), ((), ())), preferred_element_type=jnp.float32
    )
    sigmoid_in = jax.nn.sigmoid(act_in)
    dact = (dhidden * sigmoid_in * (1.0 + act_in * (1.0 - sigmoid_in))).astype(jnp.bfloat16)
    grad_in = lax.dot_general(
        edges, dact, (((0,), (0,)), ((), ())), preferred_element_type=jnp.float32
    )
    grad_out = lax.dot_general(
        hidden_head, dpred, (((0,), (1,)), ((), ())), preferred_element_type=jnp.float32
    )
    grad_in, grad_out = lax.psum((grad_in, grad_out), ("rep", "gx", "gy"))
    return (nodes, grad_in, grad_out)


def solution(mesh):
    return jax.shard_map(
        body,
        mesh=mesh,
        in_specs=(
            P(("rep", "gx", "gy"), None),
            P(("rep", "gx", "gy"), None),
            P(("rep", "gx", "gy")),
            P(("rep", "gx", "gy")),
            P(("rep", "gx", "gy")),
            P("rep", "gx", "gy", None, None, None),
            P(),
            P(),
            P(),
            P(),
            P(),
            P(None, ("rep", "gx", "gy")),
        ),
        out_specs=(P(("rep", "gx", "gy"), None), P(), P()),
        check_vma=False,
    )
```

profile of v0, /device:TPU:0, one launch (start us, length us, event | category | flops | bytes accessed | tf_op | source)
XLA Modules:
  0.0 327.0 jit_solution(12052585623107970386)
XLA Ops:
  8.2 1.9 gather_fusion
  10.1 3.0 collective-permute-start
  18.9 1.6 collective-permute-start.2
  21.1 2.2 collective-permute-start.3
  23.4 3.5 %collective-permute-done.2 = bf16[4,1,64,256]{3,2,1,0:T(8,128)(2,1)S(1)} collective-permute-done((bf16[4,1,64,256]{3,2,1,0:T(8,128)(2,1)S(1)}, bf16[4,1,64,256]{3,2,1,0:T(8,128)(2,1)S(1)}, u32[]{:S(2)}, u32[]{:S(2)}) %collective-permute-start.2) | collective-permute-done | bytes 131104 | tf_op jit(solution)/shard_map/ppermute | solution.py:31
  31.4 2.2 broadcast.102.clone
  33.7 61.8 %while.26 = (s32[]{:T(128)}, f32[256,256]{1,0:T(8,128)S(1)}, bf16[4,2048,256]{2,1,0:T(8,128)(2,1)}, s32[4,2048]{1,0:T(4,128)S(1)}, f32[4,2048,1]{1,2,0:T(1,128)S...) while((s32[]{:T(128)}, f32[256,256]{1,0:T(8,128)S(1)}, ...), condition=%wide.region_1.2_spmd.clone, body=%wide.region_0.1_spmd.clone.sunk | while | flops 4306108416 | bytes 55403708 | solution.py:84
  33.7 3.6 %fusion.83 = f32[2048,512]{1,0:T(8,128)S(1)} fusion(bf16[1024,512]{1,0:T(8,128)(2,1)} %get-tuple-element.442, s32[2048]{0:T(1024)S(1)} %bitcast.226), kind=kOutput, calls=%fused_computation.7.clone.1 | convolution fusion | flops 2149580800 | bytes 5251072 | tf_op jit(solution)/shard_map/while/body/eval_jaxpr/dot_general | solution.py:60
  39.0 2.0 copy-done.16
  41.1 2.6 bitcast_dynamic-update-slice_fusion.4
  43.7 5.5 %fusion.84 = f32[256,256]{1,0:T(8,128)S(1)} fusion(f32[2048,512]{1,0:T(8,128)} %copy-done.1, f32[2048,256]{1,0:T(8,128)} %get-tuple-element.395, f32[2048]{0:T(1024)S(1)} %bitcast.223, s32[2048]{0:T(1024)S(1)} %bitcast.219, f32[256,256]{1,0:T(8,128)S(1)} %get-tuple-element.424, pred[]{:T(512)S(6)} %compare.6), kind=kOutput, calls=%fused_computation.17.clone.1 | convolution fusion | flops 1613889536 | bytes 4734977 | tf_op jit(solution)/shard_map/while/body/eval_jaxpr/dot_general | solution.py:68
  49.2 3.6 %fusion.83 = f32[2048,512]{1,0:T(8,128)S(1)} fusion(bf16[1024,512]{1,0:T(8,128)(2,1)} %get-tuple-element.442, s32[2048]{0:T(1024)S(1)} %bitcast.226), kind=kOutput, calls=%fused_computation.7.clone.1 | convolution fusion | flops 2149580800 | bytes 5251072 | tf_op jit(solution)/shard_map/while/body/eval_jaxpr/dot_general | solution.py:60
  54.5 2.0 copy-done.16
  56.6 2.5 bitcast_dynamic-update-slice_fusion.4
  59.1 5.5 %fusion.84 = f32[256,256]{1,0:T(8,128)S(1)} fusion(f32[2048,512]{1,0:T(8,128)} %copy-done.1, f32[2048,256]{1,0:T(8,128)} %get-tuple-element.395, f32[2048]{0:T(1024)S(1)} %bitcast.223, s32[2048]{0:T(1024)S(1)} %bitcast.219, f32[256,256]{1,0:T(8,128)S(1)} %get-tuple-element.424, pred[]{:T(512)S(6)} %compare.6), kind=kOutput, calls=%fused_computation.17.clone.1 | convolution fusion | flops 1613889536 | bytes 4734977 | tf_op jit(solution)/shard_map/while/body/eval_jaxpr/dot_general | solution.py:68
  64.6 3.6 %fusion.83 = f32[2048,512]{1,0:T(8,128)S(1)} fusion(bf16[1024,512]{1,0:T(8,128)(2,1)} %get-tuple-element.442, s32[2048]{0:T(1024)S(1)} %bitcast.226), kind=kOutput, calls=%fused_computation.7.clone.1 | convolution fusion | flops 2149580800 | bytes 5251072 | tf_op jit(solution)/shard_map/while/body/eval_jaxpr/dot_general | solution.py:60
  69.9 2.0 copy-done.16
  72.0 2.6 bitcast_dynamic-update-slice_fusion.4
  74.5 5.5 %fusion.84 = f32[256,256]{1,0:T(8,128)S(1)} fusion(f32[2048,512]{1,0:T(8,128)} %copy-done.1, f32[2048,256]{1,0:T(8,128)} %get-tuple-element.395, f32[2048]{0:T(1024)S(1)} %bitcast.223, s32[2048]{0:T(1024)S(1)} %bitcast.219, f32[256,256]{1,0:T(8,128)S(1)} %get-tuple-element.424, pred[]{:T(512)S(6)} %compare.6), kind=kOutput, calls=%fused_computation.17.clone.1 | convolution fusion | flops 1613889536 | bytes 4734977 | tf_op jit(solution)/shard_map/while/body/eval_jaxpr/dot_general | solution.py:68
  80.0 3.6 %fusion.83 = f32[2048,512]{1,0:T(8,128)S(1)} fusion(bf16[1024,512]{1,0:T(8,128)(2,1)} %get-tuple-element.442, s32[2048]{0:T(1024)S(1)} %bitcast.226), kind=kOutput, calls=%fused_computation.7.clone.1 | convolution fusion | flops 2149580800 | bytes 5251072 | tf_op jit(solution)/shard_map/while/body/eval_jaxpr/dot_general | solution.py:60
  85.4 2.0 copy-done.16
  87.4 2.6 bitcast_dynamic-update-slice_fusion.4
  90.0 5.5 %fusion.84 = f32[256,256]{1,0:T(8,128)S(1)} fusion(f32[2048,512]{1,0:T(8,128)} %copy-done.1, f32[2048,256]{1,0:T(8,128)} %get-tuple-element.395, f32[2048]{0:T(1024)S(1)} %bitcast.223, s32[2048]{0:T(1024)S(1)} %bitcast.219, f32[256,256]{1,0:T(8,128)S(1)} %get-tuple-element.424, pred[]{:T(512)S(6)} %compare.6), kind=kOutput, calls=%fused_computation.17.clone.1 | convolution fusion | flops 1613889536 | bytes 4734977 | tf_op jit(solution)/shard_map/while/body/eval_jaxpr/dot_general | solution.py:68
  99.2 2.8 collective-permute-done.4
  103.8 3.6 %collective-permute-start.7 = (bf16[4,1,64,256]{3,2,1,0:T(8,128)(2,1)S(1)}, bf16[4,1,64,256]{3,2,1,0:T(8,128)(2,1)S(1)}, u32[]{:S(2)}, u32[]{:S(2)}) collective-permute-start(bf16[4,1,64,256]{3,2,1,0:T(8,128)(2,1)S(1)} %get-tuple-element.261), channel_id=1, source_target_pairs={{1,0},{2,1},{3,2},{0,3},{5,4},{6,5},{7,6},{4,7},{9,8},{10,9},{11,1... | collective-permute-start | bytes 393224 | tf_op jit(solution)/shard_map/ppermute | solution.py:32
  107.4 3.5 %collective-permute-done.6 = bf16[4,1,64,256]{3,2,1,0:T(8,128)(2,1)S(1)} collective-permute-done((bf16[4,1,64,256]{3,2,1,0:T(8,128)(2,1)S(1)}, bf16[4,1,64,256]{3,2,1,0:T(8,128)(2,1)S(1)}, u32[]{:S(2)}, u32[]{:S(2)}) %collective-permute-start.6) | collective-permute-done | bytes 131104 | tf_op jit(solution)/shard_map/ppermute | solution.py:31
  111.5 2.3 broadcast.102
  113.8 56.8 %while.27 = (s32[]{:T(128)}, f32[256,256]{1,0:T(8,128)S(1)}, bf16[4,2048,256]{2,1,0:T(8,128)(2,1)}, s32[4,2048]{1,0:T(4,128)S(1)}, f32[4,2048,1]{1,2,0:T(1,128)S...) while((s32[]{:T(128)}, f32[256,256]{1,0:T(8,128)S(1)}, ...), condition=%wide.region_5.6_spmd.clone, body=%wide.region_4.5_spmd.clone.sunk | while | flops 4306108416 | bytes 55403708 | solution.py:84
  113.8 2.4 fusion.88
  117.8 2.0 copy-done.5
  119.9 2.6 bitcast_dynamic-update-slice_fusion.5
  122.5 5.5 %fusion.89 = f32[256,256]{1,0:T(8,128)S(1)} fusion(f32[2048,512]{1,0:T(8,128)} %copy-done.2, f32[2048,256]{1,0:T(8,128)} %get-tuple-element.409, f32[2048]{0:T(1024)S(1)} %bitcast.225, s32[2048]{0:T(1024)S(1)} %bitcast.221, f32[256,256]{1,0:T(8,128)S(1)} %get-tuple-element.460, pred[]{:T(512)S(6)} %compare.7), kind=kOutput, calls=%fused_computation.41.clone.1 | convolution fusion | flops 1613889536 | bytes 4734977 | tf_op jit(solution)/shard_map/while/body/eval_jaxpr/dot_general | solution.py:68
  128.0 2.4 fusion.88
  132.1 2.0 copy-done.5
  134.1 2.5 bitcast_dynamic-update-slice_fusion.5
  136.7 5.5 %fusion.89 = f32[256,256]{1,0:T(8,128)S(1)} fusion(f32[2048,512]{1,0:T(8,128)} %copy-done.2, f32[2048,256]{1,0:T(8,128)} %get-tuple-element.409, f32[2048]{0:T(1024)S(1)} %bitcast.225, s32[2048]{0:T(1024)S(1)} %bitcast.221, f32[256,256]{1,0:T(8,128)S(1)} %get-tuple-element.460, pred[]{:T(512)S(6)} %compare.7), kind=kOutput, calls=%fused_computation.41.clone.1 | convolution fusion | flops 1613889536 | bytes 4734977 | tf_op jit(solution)/shard_map/while/body/eval_jaxpr/dot_general | solution.py:68
  142.2 2.4 fusion.88
  146.2 2.0 copy-done.5
  148.3 2.6 bitcast_dynamic-update-slice_fusion.5
  150.9 5.5 %fusion.89 = f32[256,256]{1,0:T(8,128)S(1)} fusion(f32[2048,512]{1,0:T(8,128)} %copy-done.2, f32[2048,256]{1,0:T(8,128)} %get-tuple-element.409, f32[2048]{0:T(1024)S(1)} %bitcast.225, s32[2048]{0:T(1024)S(1)} %bitcast.221, f32[256,256]{1,0:T(8,128)S(1)} %get-tuple-element.460, pred[]{:T(512)S(6)} %compare.7), kind=kOutput, calls=%fused_computation.41.clone.1 | convolution fusion | flops 1613889536 | bytes 4734977 | tf_op jit(solution)/shard_map/while/body/eval_jaxpr/dot_general | solution.py:68
  156.4 2.4 fusion.88
  160.5 2.0 copy-done.5
  162.5 2.6 bitcast_dynamic-update-slice_fusion.5
  165.1 5.5 %fusion.89 = f32[256,256]{1,0:T(8,128)S(1)} fusion(f32[2048,512]{1,0:T(8,128)} %copy-done.2, f32[2048,256]{1,0:T(8,128)} %get-tuple-element.409, f32[2048]{0:T(1024)S(1)} %bitcast.225, s32[2048]{0:T(1024)S(1)} %bitcast.221, f32[256,256]{1,0:T(8,128)S(1)} %get-tuple-element.460, pred[]{:T(512)S(6)} %compare.7), kind=kOutput, calls=%fused_computation.41.clone.1 | convolution fusion | flops 1613889536 | bytes 4734977 | tf_op jit(solution)/shard_map/while/body/eval_jaxpr/dot_general | solution.py:68
  170.6 6.9 %multiply_convert_fusion = (bf16[8192,256]{1,0:T(8,128)(2,1)S(1)}, f32[8192,256]{1,0:T(8,128)}) fusion(bf16[8192,256]{1,0:T(8,128)(2,1)} %bitcast.214, bf16[256,256]{1,0:T(8,128)(2,1)S(1)} %copy-done), kind=kOutput, calls=%fused_computation.62 | convolution fusion | flops 1084227584 | bytes 16908288 | tf_op jit(solution)/shard_map/dot_general | solution.py:134
  180.7 9.2 %fusion.40 = f32[256,256]{1,0:T(8,128)} fusion(bf16[8192,256]{1,0:T(8,128)(2,1)} %bitcast.215, bf16[169,8192]{1,0:T(8,128)(2,1)S(1)} %fusion.39, bf16[256,169]{0,1:T(8,128)(2,1)S(1)} %copy-done.18, f32[8192,256]{1,0:T(8,128)} %get-tuple-element.272), kind=kOutput, calls=%fused_computation.64 | convolution fusion | flops 1801453568 | bytes 15700480 | tf_op jit(solution)/shard_map/dot_general | solution.py:146
  191.1 125.7 %all-reduce.3.cloned.1.call-done = (f32[256,256]{1,0:T(8,128)}, f32[256,169]{0,1:T(8,128)}) async-done(((f32[256,256]{1,0:T(8,128)}, f32[256,169]{0,1:T(8,128)}), (f32[256,256]{1,0:T(8,128)}, f32[256,169]{0,1:T(8,128)})) %all-reduce.3.cloned.1.call-update) | async-done | bytes 435216 | tf_op jit(solution)/shard_map/psum | solution.py:152
  316.8 1.7 copy.60
  (156 shorter events, 36.2 us)
Async XLA Ops:
  7.2 163.4 %copy-start = (bf16[256,256]{1,0:T(8,128)(2,1)S(1)}, bf16[256,256]{1,0:T(8,128)(2,1)}, u32[]{:S(2)}) copy-start(bf16[256,256]{1,0:T(8,128)(2,1)} %param.25) | copy-start | bytes 393220
  7.2 7.2 %copy-start.3 = (bf16[256,256]{1,0:T(8,128)(2,1)S(1)}, bf16[256,256]{1,0:T(8,128)(2,1)}, u32[]{:S(2)}) copy-start(bf16[256,256]{1,0:T(8,128)(2,1)} %param.16) | copy-start | bytes 393220
  7.2 7.2 %copy-start.6 = (bf16[2,256,768]{2,1,0:T(8,128)(2,1)S(1)}, bf16[2,256,768]{2,1,0:T(8,128)(2,1)}, u32[]{:S(2)}) copy-start(bf16[2,256,768]{2,1,0:T(8,128)(2,1)} %param.22) | copy-start | bytes 2359300
  7.2 8.1 %copy-start.7 = (bf16[2,256,256]{2,1,0:T(8,128)(2,1)S(1)}, bf16[2,256,256]{2,1,0:T(8,128)(2,1)}, u32[]{:S(2)}) copy-start(bf16[2,256,256]{2,1,0:T(8,128)(2,1)} %param.23) | copy-start | bytes 786436
  7.2 8.9 %copy-start.12 = (s32[8192]{0:T(1024)S(1)}, s32[8192]{0:T(1024)}, u32[]{:S(2)}) copy-start(s32[8192]{0:T(1024)} %param.19) | copy-start | bytes 98308
  7.2 8.9 %copy-start.13 = (s32[8192]{0:T(1024)S(1)}, s32[8192]{0:T(1024)}, u32[]{:S(2)}) copy-start(s32[8192]{0:T(1024)} %param.18) | copy-start | bytes 98308
  7.2 309.6 %all-reduce.3.cloned.1.call-start = ((), (), s32[]{:S(2)}) async-start(), calls=%async_computation | async-start | bytes 884736 | tf_op jit(solution)/shard_map/psum | solution.py:152
  10.0 10.5 %copy-start.15 = (f32[2,256]{1,0:T(2,128)S(1)}, f32[2,256]{1,0:T(2,128)}, u32[]{:S(2)}) copy-start(f32[2,256]{1,0:T(2,128)} %param.24) | copy-start | bytes 6148
  10.1 6.1 %collective-permute-start = (bf16[1,2,64,256]{3,2,1,0:T(8,128)(2,1)S(1)}, bf16[1,2,64,256]{3,2,1,0:T(8,128)(2,1)S(1)}, u32[]{:S(2)}, u32[]{:S(2)}) collective-permute-start(bf16[1,2,64,256]{3,2,1,0:T(8,128)(2,1)S(1)} %bitcast.229), channel_id=1, source_target_pairs={{0,4},{4,0},{1,5},{5,1},{2,6},{6,2},{3,7},{7,3},{8,12},{12,8},{9,1... | collective-permute-start | bytes 196616 | tf_op jit(solution)/shard_map/ppermute | solution.py:31
  13.1 4.3 %collective-permute-start.1 = (bf16[1,2,64,256]{3,2,1,0:T(8,128)(2,1)S(1)}, bf16[1,2,64,256]{3,2,1,0:T(8,128)(2,1)S(1)}, u32[]{:S(2)}, u32[]{:S(2)}) collective-permute-start(bf16[1,2,64,256]{3,2,1,0:T(8,128)(2,1)S(1)} %bitcast.228), channel_id=1, source_target_pairs={{4,0},{0,4},{5,1},{1,5},{6,2},{2,6},{7,3},{3,7},{12,8},{8,12},{13,... | collective-permute-start | bytes 196616 | tf_op jit(solution)/shard_map/ppermute | solution.py:32
  14.7 16.8 %copy-start.4 = (bf16[256,768]{1,0:T(8,128)(2,1)}, bf16[256,768]{1,0:T(8,128)(2,1)S(1)}, u32[]{:S(2)}) copy-start(bf16[256,768]{1,0:T(8,128)(2,1)S(1)} %convolution_convert_fusion.3) | copy-start | bytes 1179652
  16.2 1.2 copy-start.9
  17.4 0.6 copy-start.8
  18.9 7.9 %collective-permute-start.2 = (bf16[4,1,64,256]{3,2,1,0:T(8,128)(2,1)S(1)}, bf16[4,1,64,256]{3,2,1,0:T(8,128)(2,1)S(1)}, u32[]{:S(2)}, u32[]{:S(2)}) collective-permute-start(bf16[4,1,64,256]{3,2,1,0:T(8,128)(2,1)S(1)} %get-tuple-element.264), channel_id=1, source_target_pairs={{0,1},{1,2},{2,3},{3,0},{4,5},{5,6},{6,7},{7,4},{8,9},{9,10},{10,1... | collective-permute-start | bytes 393224 | tf_op jit(solution)/shard_map/ppermute | solution.py:31
  21.1 7.3 %collective-permute-start.3 = (bf16[4,1,64,256]{3,2,1,0:T(8,128)(2,1)S(1)}, bf16[4,1,64,256]{3,2,1,0:T(8,128)(2,1)S(1)}, u32[]{:S(2)}, u32[]{:S(2)}) collective-permute-start(bf16[4,1,64,256]{3,2,1,0:T(8,128)(2,1)S(1)} %get-tuple-element.263), channel_id=1, source_target_pairs={{1,0},{2,1},{3,2},{0,3},{5,4},{6,5},{7,6},{4,7},{9,8},{10,9},{11,1... | collective-permute-start | bytes 393224 | tf_op jit(solution)/shard_map/ppermute | solution.py:32
  30.4 3.3 %copy-start.11 = (bf16[256,256]{1,0:T(8,128)(2,1)S(1)}, bf16[256,256]{1,0:T(8,128)(2,1)}, u32[]{:S(2)}) copy-start(bf16[256,256]{1,0:T(8,128)(2,1)} %get-tuple-element.420) | copy-start | bytes 393220
  31.4 2.2 slice-start
  37.3 6.3 %copy-start.1 = (f32[2048,512]{1,0:T(8,128)}, f32[2048,512]{1,0:T(8,128)S(1)}, u32[]{:S(2)}) copy-start(f32[2048,512]{1,0:T(8,128)S(1)} %fusion.83) | copy-start | bytes 12582916 | tf_op jit(solution)/shard_map/while
  37.4 3.7 %copy-start.16 = (bf16[4,2048,256]{2,1,0:T(8,128)(2,1)S(1)}, bf16[4,2048,256]{2,1,0:T(8,128)(2,1)}, u32[]{:S(2)}) copy-start(bf16[4,2048,256]{2,1,0:T(8,128)(2,1)} %get-tuple-element.443) | copy-start | bytes 12582916 | tf_op jit(solution)/shard_map/while
  52.8 6.3 %copy-start.1 = (f32[2048,512]{1,0:T(8,128)}, f32[2048,512]{1,0:T(8,128)S(1)}, u32[]{:S(2)}) copy-start(f32[2048,512]{1,0:T(8,128)S(1)} %fusion.83) | copy-start | bytes 12582916 | tf_op jit(solution)/shard_map/while
  52.8 3.7 %copy-start.16 = (bf16[4,2048,256]{2,1,0:T(8,128)(2,1)S(1)}, bf16[4,2048,256]{2,1,0:T(8,128)(2,1)}, u32[]{:S(2)}) copy-start(bf16[4,2048,256]{2,1,0:T(8,128)(2,1)} %get-tuple-element.443) | copy-start | bytes 12582916 | tf_op jit(solution)/shard_map/while
  68.2 6.3 %copy-start.1 = (f32[2048,512]{1,0:T(8,128)}, f32[2048,512]{1,0:T(8,128)S(1)}, u32[]{:S(2)}) copy-start(f32[2048,512]{1,0:T(8,128)S(1)} %fusion.83) | copy-start | bytes 12582916 | tf_op jit(solution)/shard_map/while
  68.3 3.7 %copy-start.16 = (bf16[4,2048,256]{2,1,0:T(8,128)(2,1)S(1)}, bf16[4,2048,256]{2,1,0:T(8,128)(2,1)}, u32[]{:S(2)}) copy-start(bf16[4,2048,256]{2,1,0:T(8,128)(2,1)} %get-tuple-element.443) | copy-start | bytes 12582916 | tf_op jit(solution)/shard_map/while
  83.7 6.3 %copy-start.1 = (f32[2048,512]{1,0:T(8,128)}, f32[2048,512]{1,0:T(8,128)S(1)}, u32[]{:S(2)}) copy-start(f32[2048,512]{1,0:T(8,128)S(1)} %fusion.83) | copy-start | bytes 12582916 | tf_op jit(solution)/shard_map/while
  83.7 3.7 %copy-start.16 = (bf16[4,2048,256]{2,1,0:T(8,128)(2,1)S(1)}, bf16[4,2048,256]{2,1,0:T(8,128)(2,1)}, u32[]{:S(2)}) copy-start(bf16[4,2048,256]{2,1,0:T(8,128)(2,1)} %get-tuple-element.443) | copy-start | bytes 12582916 | tf_op jit(solution)/shard_map/while
  97.1 4.9 %collective-permute-start.4 = (bf16[1,2,64,256]{3,2,1,0:T(8,128)(2,1)S(1)}, bf16[1,2,64,256]{3,2,1,0:T(8,128)(2,1)S(1)}, u32[]{:S(2)}, u32[]{:S(2)}) collective-permute-start(bf16[1,2,64,256]{3,2,1,0:T(8,128)(2,1)S(1)} %bitcast.231), channel_id=1, source_target_pairs={{0,4},{4,0},{1,5},{5,1},{2,6},{6,2},{3,7},{7,3},{8,12},{12,8},{9,1... | collective-permute-start | bytes 196616 | tf_op jit(solution)/shard_map/ppermute | solution.py:31
  98.6 4.3 %collective-permute-start.5 = (bf16[1,2,64,256]{3,2,1,0:T(8,128)(2,1)S(1)}, bf16[1,2,64,256]{3,2,1,0:T(8,128)(2,1)S(1)}, u32[]{:S(2)}, u32[]{:S(2)}) collective-permute-start(bf16[1,2,64,256]{3,2,1,0:T(8,128)(2,1)S(1)} %bitcast.230), channel_id=1, source_target_pairs={{4,0},{0,4},{5,1},{1,5},{6,2},{2,6},{7,3},{3,7},{12,8},{8,12},{13,... | collective-permute-start | bytes 196616 | tf_op jit(solution)/shard_map/ppermute | solution.py:32
  102.9 7.9 %collective-permute-start.6 = (bf16[4,1,64,256]{3,2,1,0:T(8,128)(2,1)S(1)}, bf16[4,1,64,256]{3,2,1,0:T(8,128)(2,1)S(1)}, u32[]{:S(2)}, u32[]{:S(2)}) collective-permute-start(bf16[4,1,64,256]{3,2,1,0:T(8,128)(2,1)S(1)} %get-tuple-element.262), channel_id=1, source_target_pairs={{0,1},{1,2},{2,3},{3,0},{4,5},{5,6},{6,7},{7,4},{8,9},{9,10},{10,1... | collective-permute-start | bytes 393224 | tf_op jit(solution)/shard_map/ppermute | solution.py:31
  103.8 7.1 %collective-permute-start.7 = (bf16[4,1,64,256]{3,2,1,0:T(8,128)(2,1)S(1)}, bf16[4,1,64,256]{3,2,1,0:T(8,128)(2,1)S(1)}, u32[]{:S(2)}, u32[]{:S(2)}) collective-permute-start(bf16[4,1,64,256]{3,2,1,0:T(8,128)(2,1)S(1)} %get-tuple-element.261), channel_id=1, source_target_pairs={{1,0},{2,1},{3,2},{0,3},{5,4},{6,5},{7,6},{4,7},{9,8},{10,9},{11,1... | collective-permute-start | bytes 393224 | tf_op jit(solution)/shard_map/ppermute | solution.py:32
  111.4 2.4 copy-start.10
  116.2 6.3 %copy-start.2 = (f32[2048,512]{1,0:T(8,128)}, f32[2048,512]{1,0:T(8,128)S(1)}, u32[]{:S(2)}) copy-start(f32[2048,512]{1,0:T(8,128)S(1)} %fusion.88) | copy-start | bytes 12582916 | tf_op jit(solution)/shard_map/while
  116.2 3.7 %copy-start.5 = (bf16[4,2048,256]{2,1,0:T(8,128)(2,1)S(1)}, bf16[4,2048,256]{2,1,0:T(8,128)(2,1)}, u32[]{:S(2)}) copy-start(bf16[4,2048,256]{2,1,0:T(8,128)(2,1)} %get-tuple-element.479) | copy-start | bytes 12582916 | tf_op jit(solution)/shard_map/while
  130.4 6.2 %copy-start.2 = (f32[2048,512]{1,0:T(8,128)}, f32[2048,512]{1,0:T(8,128)S(1)}, u32[]{:S(2)}) copy-start(f32[2048,512]{1,0:T(8,128)S(1)} %fusion.88) | copy-start | bytes 12582916 | tf_op jit(solution)/shard_map/while
  130.4 3.7 %copy-start.5 = (bf16[4,2048,256]{2,1,0:T(8,128)(2,1)S(1)}, bf16[4,2048,256]{2,1,0:T(8,128)(2,1)}, u32[]{:S(2)}) copy-start(bf16[4,2048,256]{2,1,0:T(8,128)(2,1)} %get-tuple-element.479) | copy-start | bytes 12582916 | tf_op jit(solution)/shard_map/while
  144.6 6.3 %copy-start.2 = (f32[2048,512]{1,0:T(8,128)}, f32[2048,512]{1,0:T(8,128)S(1)}, u32[]{:S(2)}) copy-start(f32[2048,512]{1,0:T(8,128)S(1)} %fusion.88) | copy-start | bytes 12582916 | tf_op jit(solution)/shard_map/while
  144.6 3.7 %copy-start.5 = (bf16[4,2048,256]{2,1,0:T(8,128)(2,1)S(1)}, bf16[4,2048,256]{2,1,0:T(8,128)(2,1)}, u32[]{:S(2)}) copy-start(bf16[4,2048,256]{2,1,0:T(8,128)(2,1)} %get-tuple-element.479) | copy-start | bytes 12582916 | tf_op jit(solution)/shard_map/while
  158.8 6.3 %copy-start.2 = (f32[2048,512]{1,0:T(8,128)}, f32[2048,512]{1,0:T(8,128)S(1)}, u32[]{:S(2)}) copy-start(f32[2048,512]{1,0:T(8,128)S(1)} %fusion.88) | copy-start | bytes 12582916 | tf_op jit(solution)/shard_map/while
  158.8 3.7 %copy-start.5 = (bf16[4,2048,256]{2,1,0:T(8,128)(2,1)S(1)}, bf16[4,2048,256]{2,1,0:T(8,128)(2,1)}, u32[]{:S(2)}) copy-start(bf16[4,2048,256]{2,1,0:T(8,128)(2,1)} %get-tuple-element.479) | copy-start | bytes 12582916 | tf_op jit(solution)/shard_map/while
  170.6 6.9 %copy-start.17 = (bf16[169,8192]{1,0:T(8,128)(2,1)S(1)}, bf16[169,8192]{1,0:T(8,128)(2,1)}, u32[]{:S(2)}) copy-start(bf16[169,8192]{1,0:T(8,128)(2,1)} %param.27) | copy-start | bytes 8306692
  170.6 6.9 %copy-start.18 = (bf16[256,169]{0,1:T(8,128)(2,1)S(1)}, bf16[256,169]{0,1:T(8,128)(2,1)}, u32[]{:S(2)}) copy-start(bf16[256,169]{0,1:T(8,128)(2,1)} %param.26) | copy-start | bytes 259588
  180.7 9.6 %copy-start.14 = (f32[1,256]{1,0:T(1,128)S(1)}, f32[1,256]{1,0:T(1,128)}, u32[]{:S(2)}) copy-start(f32[1,256]{1,0:T(1,128)} %get-tuple-element.269) | copy-start | bytes 3076
Sparse Core Ops, SparseCore 0:
  190.4 126.3 all-reduce.2
where the time goes:
time: 329 us; the launch traced here: 327 us
  waiting for transfers between devices  138 us (42%)
  matrix products  122 us (37%)
  local copies, waits for them, and re-layouts  34 us (10%)
  between operations  15.2 us (5%)
  starting transfers between devices  13.2 us (4%)
  other arithmetic  4.45 us (1%)
    psum x1, waiting for transfers between devices, body(): grad_in, grad_out = lax.psum((grad_in, grad_out), ('rep', 'gx', 'gy'))  126 us
    dot_general x8, matrix products, one_block(): lax.dot_general(target_hot.astype(jnp.float32), weighted, (((0,), (0,)),...  43.7 us
    dot_general x8, matrix products, one_block(): gathered = jnp.dot(source_hot, table, preferred_element_type=jnp.float32)  24.1 us
    dot_general x8, matrix products, one_block(): jnp.dot(edge_rows, weight_edge, preferred_element_type=jnp.float32)  20.7 us
    while x32, local copies, waits for them, and re-layouts  16.4 us
    dot_general x8, matrix products, one_block(): jnp.dot(target_hot, query_part, preferred_element_type=jnp.float32)  13 us
    ppermute x4, waiting for transfers between devices, with_halo(): before = lax.ppermute(last, axis, up)  9.83 us
    dot_general x1, matrix products, body(): lax.dot_general(edges, dact, (((0,), (0,)), ((), ())), preferred_element_...  9.24 us
  transfers between devices with their start and end apart: 9, of which 6 were waited for; matrix products, arithmetic and copies ran while one was open for 2% of the time, Pallas kernels for 0%

commit v1 on v0

v1 whole, which is shorter than its diff:
```python
import functools

import jax
import jax.numpy as jnp
from jax import lax
from jax.experimental import pallas as pl
from jax.experimental.pallas import tpu as pltpu
from jax.sharding import PartitionSpec as P

F32 = jnp.float32
BF16 = jnp.bfloat16
BLOCK = 1024
SUB = 512
CELLS = tuple((i, j) for i in range(4) for j in range(4) if not (i in (1, 2) and j in (1, 2)))
NT = (((1,), (1,)), ((), ()))


def nn(a, b):
    return jnp.dot(a, b, preferred_element_type=F32)


def nt(a, b):
    return lax.dot_general(a, b, NT, preferred_element_type=F32)


def sigmoid(v):
    return 0.5 * jnp.tanh(0.5 * v) + 0.5


def hot(rows_iota, row, base):
    picked = jnp.where((row >= base) & (row < base + 256), row - base, -1)
    picked = picked.astype(F32).astype(BF16)
    return jnp.where(rows_iota == picked, jnp.ones((), BF16), jnp.zeros((), BF16))


def fill_tables(nodes, ghosts, w_qkv, kv_t, q_t):
    atoms = nodes.shape[0]
    w_t = w_qkv.T
    q_t[...] = nt(w_t[:256], nodes).astype(BF16)
    kv_t[:, :atoms] = nt(w_t[256:], nodes).astype(BF16)
    kv_t[:, atoms:] = nt(w_t[256:], ghosts).astype(BF16)


def edge_step(edges_t, src, dst, live, iota, kv_t, q_t, we_t):
    dst_hot = hot(iota, dst, 0)
    table_rows = kv_t.shape[1]
    gathered = nn(kv_t[:, :256], hot(iota, src, 0))
    for base in range(256, table_rows, 256):
        gathered = gathered + nn(kv_t[:, base : base + 256], hot(iota, src, base))
    pre = gathered[:256] + nn(q_t[...], dst_hot) + nn(we_t[...], edges_t)
    gate = live * sigmoid(pre)
    new_edges = (edges_t.astype(F32) + gate * pre).astype(BF16)
    weighted = gate * gathered[256:]
    high = weighted.astype(BF16)
    low = (weighted - high.astype(F32)).astype(BF16)
    added = nt(jnp.concatenate([high, low], axis=0), dst_hot)
    return new_edges, added[:256] + added[256:]


def update_nodes(nodes, summed_t, gain):
    summed = summed_t.T
    centre = summed - jnp.mean(summed, axis=-1, keepdims=True)
    spread = jnp.mean(centre * centre, axis=-1, keepdims=True)
    return (nodes.astype(F32) + gain * (centre * lax.rsqrt(spread + 1e-05))).astype(BF16)


def layer_kernel(
    layer, scale, count, nodes, ghosts, w_qkv, w_edge, gains, edges, src, dst, *rest
):
    last = scale is not None
    if last:
        head_in, head_out, targets, out_nodes, grad_in, grad_out = rest[:6]
        kv_t, q_t, we_t, iota, summed, head_in_t, head_out_t = rest[6:]
    else:
        out_nodes, out_edges = rest[:2]
        kv_t, q_t, we_t, iota, summed = rest[2:]
    step = pl.program_id(0)

    @pl.when(step == 0)
    def _():
        fill_tables(nodes[...], ghosts[...], w_qkv[0], kv_t, q_t)
        we_t[...] = w_edge[0].T
        iota[...] = lax.broadcasted_iota(jnp.int32, iota.shape, 0).astype(F32).astype(BF16)
        summed[...] = jnp.zeros_like(summed)
        if last:
            head_in_t[...] = head_in[...].T
            head_out_t[...] = head_out[...].T
            grad_in[...] = jnp.zeros_like(grad_in)
            grad_out[...] = jnp.zeros_like(grad_out)

    for part in range(BLOCK // SUB):
        lanes = slice(part * SUB, (part + 1) * SUB)
        position = step * BLOCK + part * SUB + lax.broadcasted_iota(jnp.int32, (1, SUB), 1)
        live = jnp.where(position < count[0], 1.0, 0.0).astype(F32)
        edges_t = edges[:, lanes] if last else edges[lanes, :].T
        new_edges, added = edge_step(
            edges_t, src[:, lanes], dst[:, lanes], live, iota[...], kv_t, q_t, we_t
        )
        summed[...] += added
        if not last:
            out_edges[:, lanes] = new_edges
            continue
        act = nn(head_in_t[...], new_edges)
        sig = sigmoid(act)
        hidden = (act * sig).astype(BF16)
        pred = nn(head_out_t[...], hidden)
        dpred = (live * (pred - targets[:, lanes].astype(F32)) * scale).astype(BF16)
        dhidden = nn(head_out[...], dpred)
        dact = (dhidden * sig * (1.0 + act * (1.0 - sig))).astype(BF16)
        grad_in[...] += nt(new_edges, dact)
        grad_out[...] += nt(hidden, dpred)

    @pl.when(step == pl.num_programs(0) - 1)
    def _():
        out_nodes[...] = update_nodes(nodes[...], summed[...], gains[layer : layer + 1, :])


def run_layer(layer, scale, count, nodes, ghosts, w_qkv, w_edge, gains, edges, src, dst, heads):
    atoms, width = nodes.shape
    slots = src.shape[1]
    last = scale is not None
    whole = lambda a: pl.BlockSpec(a.shape, lambda i: (0,) * a.ndim)
    by_layer = lambda a: pl.BlockSpec((1,) + a.shape[1:], lambda i: (layer, 0, 0))
    lanes = lambda rows: pl.BlockSpec((rows, BLOCK), lambda i: (0, i))
    edge_spec = lanes(width) if last else pl.BlockSpec((BLOCK, width), lambda i: (i, 0))
    in_specs = [
        pl.BlockSpec(memory_space=pltpu.SMEM),
        whole(nodes),
        whole(ghosts),
        by_layer(w_qkv),
        by_layer(w_edge),
        whole(gains),
        edge_spec,
        lanes(1),
        lanes(1),
    ]
    out_shape = [jax.ShapeDtypeStruct(nodes.shape, BF16)]
    out_specs = [pl.BlockSpec((atoms, width), lambda i: (0, 0))]
    table_rows = atoms + ghosts.shape[0]
    scratch = [
        pltpu.VMEM((2 * width, table_rows), BF16),
        pltpu.VMEM((width, atoms), BF16),
        pltpu.VMEM((width, width), BF16),
        pltpu.VMEM((256, SUB), BF16),
        pltpu.VMEM((width, atoms), F32),
    ]
    operands = [count, nodes, ghosts, w_qkv, w_edge, gains, edges, src, dst]
    if last:
        head_in, head_out, targets = heads
        operands += list(heads)
        in_specs += [whole(head_in), whole(head_out), lanes(targets.shape[0])]
        for like in (head_in, head_out):
            out_shape.append(jax.ShapeDtypeStruct(like.shape, F32))
            out_specs.append(whole(like))
        scratch += [
            pltpu.VMEM(head_in.shape[::-1], BF16),
            pltpu.VMEM(head_out.shape[::-1], BF16),
        ]
    else:
        out_shape.append(jax.ShapeDtypeStruct((width, slots), BF16))
        out_specs.append(lanes(width))
    return pl.pallas_call(
        functools.partial(layer_kernel, layer, scale),
        grid=(slots // BLOCK,),
        in_specs=in_specs,
        out_specs=out_specs,
        out_shape=out_shape,
        scratch_shapes=scratch,
        compiler_params=pltpu.CompilerParams(
            dimension_semantics=("arbitrary",), vmem_limit_bytes=48 << 20
        ),
    )(*operands)


def with_halo(x, sides, width):
    for axis, dim in sides:
        count, length = (lax.axis_size(axis), x.shape[dim])
        up = [(i, (i + 1) % count) for i in range(count)]
        down = [(j, i) for i, j in up]
        last = lax.slice_in_dim(x, length - width, length, axis=dim)
        initial = lax.slice_in_dim(x, 0, width, axis=dim)
        before = lax.ppermute(last, axis, up)
        after = lax.ppermute(initial, axis, down)
        x = jnp.concatenate([before, x, after], axis=dim)
    return x


def exchange(nodes, corner_index):
    padded = with_halo(nodes[corner_index], (("gx", 0), ("gy", 1)), 1)
    return jnp.concatenate([padded[i, j] for i, j in CELLS], axis=0)


def body(
    node_feat,
    edge_feat,
    edge_src,
    edge_dst,
    edge_count,
    send_idx,
    w_qkv,
    w_edge,
    gains,
    head_in,
    head_out,
    targets,
):
    slots = edge_feat.shape[0]
    layers = w_qkv.shape[0]
    corner_index = send_idx.reshape(2, 2, send_idx.shape[-1])
    src = edge_src.reshape(1, slots)
    dst = edge_dst.reshape(1, slots)
    scale = 0.125 / (slots * lax.axis_size(("rep", "gx", "gy"))) ** 0.5
    nodes = node_feat
    edges = edge_feat
    for layer in range(layers):
        ghosts = exchange(nodes, corner_index)
        last = layer == layers - 1
        outs = run_layer(
            layer,
            scale if last else None,
            edge_count,
            nodes,
            ghosts,
            w_qkv,
            w_edge,
            gains,
            edges,
            src,
            dst,
            (head_in, head_out, targets),
        )
        if last:
            nodes, grad_in, grad_out = outs
        else:
            nodes, edges = outs
    grad_in, grad_out = lax.psum((grad_in, grad_out), ("rep", "gx", "gy"))
    return (nodes, grad_in, grad_out)


def solution(mesh):
    tiles = ("rep", "gx", "gy")
    return jax.shard_map(
        body,
        mesh=mesh,
        in_specs=(
            P(tiles, None),
            P(tiles, None),
            P(tiles),
            P(tiles),
            P(tiles),
            P("rep", "gx", "gy", None, None, None),
            P(),
            P(),
            P(),
            P(),
            P(),
            P(None, tiles),
        ),
        out_specs=(P(tiles, None), P(), P()),
        check_vma=False,
    )
```

time: 329 us -> 241 us (0.73)
  matrix products: 122 us -> 0 us
  Pallas kernels: 0 us -> 51.4 us
  local copies, waits for them, and re-layouts: 34 us -> 15.8 us
  waiting for transfers between devices: 138 us -> 144 us
  other arithmetic: 4.45 us -> 0.76 us
    dot_general x40 -> x0, matrix products: 122 us -> none  [the longest x8 43.7 us: one_block(): lax.dot_general(target_hot.astype(jnp.float32), weighted, (((0,), (0,)),...]
    pallas_call x0 -> x2, Pallas kernels: none -> 51.4 us  [run_layer(): pl.pallas_call(functools.partial(layer_kernel, layer, scale), grid=(slots...]
    while x32 -> x0, local copies, waits for them, and re-layouts: 16.4 us -> none
    unnamed x54 -> x55, local copies, waits for them, and re-layouts: 7.1 us -> 12.6 us
    another operation x2 -> x0, local copies, waits for them, and re-layouts: 4.51 us -> none
  transfers between devices with their start and end apart: 9 -> 9, of which waited for: 6 -> 8; matrix products, arithmetic and copies ran while one was open for 2% -> 0% of each run, Pallas kernels for 0% -> 0%
where the time goes in v1:
time: 241 us; the launch traced here: 240 us
  waiting for transfers between devices  144 us (60%)
  Pallas kernels  51.4 us (21%)
  local copies, waits for them, and re-layouts  15.8 us (7%)
  between operations  15 us (6%)
  starting transfers between devices  13.1 us (5%)
    psum x1, waiting for transfers between devices, body(): grad_in, grad_out = lax.psum((grad_in, grad_out), ('rep', 'gx', 'gy'))  129 us
    pallas_call x2, Pallas kernels, run_layer(): pl.pallas_call(functools.partial(layer_kernel, layer, scale), grid=(slots...  51.4 us
    unnamed x55, local copies, waits for them, and re-layouts  12.6 us
    ppermute x4, waiting for transfers between devices, with_halo(): before = lax.ppermute(last, axis, up)  11.4 us
    ppermute x4, starting transfers between devices, with_halo(): after = lax.ppermute(initial, axis, down)  7.07 us
    ppermute x4, starting transfers between devices, with_halo(): before = lax.ppermute(last, axis, up)  5.99 us
  transfers between devices with their start and end apart: 9, of which 8 were waited for; matrix products, arithmetic and copies ran while one was open for 0% of the time, Pallas kernels for 0%

profile of v1, /device:TPU:0, one launch (start us, length us, event | category | flops | bytes accessed | tf_op | source)
XLA Modules:
  0.0 240.3 jit_solution(548168150643305538)
XLA Ops:
  7.2 0.0 all-reduce.3.cloned.1.call-start
  7.2 0.7 compare_select_fusion
  7.9 0.1 reshape.48
  8.0 1.9 gather_fusion
  9.9 3.0 %collective-permute-start = (bf16[1,2,64,256]{3,2,1,0:T(8,128)(2,1)S(1)}, bf16[1,2,64,256]{3,2,1,0:T(8,128)(2,1)S(1)}, u32[]{:S(2)}, u32[]{:S(2)}) collective-permute-start(bf16[1,2,64,256]{3,2,1,0:T(8,128)(2,1)S(1)} %bitcast.116), channel_id=1, source_target_pairs={{0,4},{4,0},{1,5},{5,1},{2,6},{6,2},{3,7},{7,3},{8,12},{12,8},{9,1... | collective-permute-start | bytes 196616 | tf_op jit(solution)/shard_map/ppermute | solution.py:182
  12.9 0.1 collective-permute-start.1
  13.0 2.3 collective-permute-done
  15.3 1.9 collective-permute-done.1
  17.3 1.6 collective-permute-start.2
  19.5 2.3 collective-permute-start.3
  21.8 3.3 %collective-permute-done.2 = bf16[4,1,64,256]{3,2,1,0:T(8,128)(2,1)S(1)} collective-permute-done((bf16[4,1,64,256]{3,2,1,0:T(8,128)(2,1)S(1)}, bf16[4,1,64,256]{3,2,1,0:T(8,128)(2,1)S(1)}, u32[]{:S(2)}, u32[]{:S(2)}) %collective-permute-start.2) | collective-permute-done | bytes 131104 | tf_op jit(solution)/shard_map/ppermute | solution.py:182
  25.1 1.4 collective-permute-done.3
  26.6 0.0 copy-start.14
  26.7 0.0 copy-start
  26.7 0.9 copy-done
  27.6 1.1 copy-done.2
  28.7 0.9 copy-done.5
  29.7 0.8 copy-done.8
  30.5 0.8 copy-done.10
  31.2 0.7 copy-done.12
  31.9 0.0 copy-start.11
  31.9 0.0 copy-start.13
  31.9 20.1 %shard_map.139 = (bf16[256,256]{1,0:T(8,128)(2,1)S(1)}, bf16[256,8192]{1,0:T(8,128)(2,1)S(1)}) custom-call(s32[1]{0:T(128)S(6)} %copy.41.count, bf16[256,256]{1,0:T(8,128)(2,1)S(1)} %copy-done, bf16[768,256]{1,0:T(8,128)(2,1)S(1)} %constant_dynamic-update-slice_fusion.ghosts, bf16[2,256,768]{2,1,0:T(8,128)(2,1)S(1)} %copy-done.2, ...), custom_call_target="tpu_custom_call" | custom-call | tf_op jit(solution)/shard_map/pallas_call | solution.py:162
  52.1 0.0 copy-start.1
  52.1 2.0 copy-done.1
  54.1 1.1 gather_fusion.1
  55.2 0.8 collective-permute-start.4
  56.0 1.3 collective-permute-start.5
  57.3 2.3 collective-permute-done.4
  59.7 0.7 collective-permute-done.5
  60.4 0.5 collective-permute-start.6
  61.0 0.0 copy-done.14
  61.0 0.1 copy.15.rest_1_
  61.1 3.4 %collective-permute-start.7 = (bf16[4,1,64,256]{3,2,1,0:T(8,128)(2,1)S(1)}, bf16[4,1,64,256]{3,2,1,0:T(8,128)(2,1)S(1)}, u32[]{:S(2)}, u32[]{:S(2)}) collective-permute-start(bf16[4,1,64,256]{3,2,1,0:T(8,128)(2,1)S(1)} %get-tuple-element.18), channel_id=1, source_target_pairs={{1,0},{2,1},{3,2},{0,3},{5,4},{6,5},{7,6},{4,7},{9,8},{10,9},{11,1... | collective-permute-start | bytes 393224 | tf_op jit(solution)/shard_map/ppermute | solution.py:183
  64.5 3.5 %collective-permute-done.6 = bf16[4,1,64,256]{3,2,1,0:T(8,128)(2,1)S(1)} collective-permute-done((bf16[4,1,64,256]{3,2,1,0:T(8,128)(2,1)S(1)}, bf16[4,1,64,256]{3,2,1,0:T(8,128)(2,1)S(1)}, u32[]{:S(2)}, u32[]{:S(2)}) %collective-permute-start.6) | collective-permute-done | bytes 131104 | tf_op jit(solution)/shard_map/ppermute | solution.py:182
  68.0 0.0 collective-permute-done.7
  68.1 0.0 copy-done.3
  68.1 0.0 copy-done.6
  68.1 0.0 copy-done.7
  68.1 0.0 copy-done.9
  68.1 0.0 copy-done.11
  68.2 0.0 copy-start.4
  68.2 1.8 copy-done.4
  70.0 31.3 %shard_map.140 = (bf16[256,256]{1,0:T(8,128)(2,1)}, f32[256,256]{1,0:T(8,128)}, f32[256,169]{1,0:T(8,128)}) custom-call(s32[1]{0:T(128)S(6)} %copy.41.count, bf16[256,256]{1,0:T(8,128)(2,1)S(1)} %get-tuple-element.8.nodes, bf16[768,256]{1,0:T(8,128)(2,1)S(1)} %constant_dynamic-update-slice_fusion.12.ghosts, bf16[2,256,768]{2,1,0:T(8,128)(2,1)S(1)} %copy-done.3, ...), custom_call_target="tpu_custom_call" | custom-call | tf_op jit(solution)/shard_map/pallas_call | solution.py:162
  101.2 0.0 all-reduce.3.cloned.1.call-update
  101.3 128.8 %all-reduce.3.cloned.1.call-done = (f32[256,256]{1,0:T(8,128)}, f32[256,169]{1,0:T(8,128)}) async-done(((f32[256,256]{1,0:T(8,128)}, f32[256,169]{1,0:T(8,128)}), (f32[256,256]{1,0:T(8,128)}, f32[256,169]{1,0:T(8,128)})) %all-reduce.3.cloned.1.call-update) | async-done | bytes 435216 | tf_op jit(solution)/shard_map/psum | solution.py:236
  230.1 1.7 copy.16
  231.8 1.7 copy.42
  (41 shorter events, 0.3 us)
Async XLA Ops:
  7.2 222.9 %all-reduce.3.cloned.1.call-start = ((), (), s32[]{:S(2)}) async-start(), calls=%async_computation | async-start | bytes 1048576 | tf_op jit(solution)/shard_map/psum | solution.py:236
  9.9 5.4 %collective-permute-start = (bf16[1,2,64,256]{3,2,1,0:T(8,128)(2,1)S(1)}, bf16[1,2,64,256]{3,2,1,0:T(8,128)(2,1)S(1)}, u32[]{:S(2)}, u32[]{:S(2)}) collective-permute-start(bf16[1,2,64,256]{3,2,1,0:T(8,128)(2,1)S(1)} %bitcast.116), channel_id=1, source_target_pairs={{0,4},{4,0},{1,5},{5,1},{2,6},{6,2},{3,7},{7,3},{8,12},{12,8},{9,1... | collective-permute-start | bytes 196616 | tf_op jit(solution)/shard_map/ppermute | solution.py:182
  12.9 4.3 %collective-permute-start.1 = (bf16[1,2,64,256]{3,2,1,0:T(8,128)(2,1)S(1)}, bf16[1,2,64,256]{3,2,1,0:T(8,128)(2,1)S(1)}, u32[]{:S(2)}, u32[]{:S(2)}) collective-permute-start(bf16[1,2,64,256]{3,2,1,0:T(8,128)(2,1)S(1)} %bitcast.114), channel_id=1, source_target_pairs={{4,0},{0,4},{5,1},{1,5},{6,2},{2,6},{7,3},{3,7},{12,8},{8,12},{13,... | collective-permute-start | bytes 196616 | tf_op jit(solution)/shard_map/ppermute | solution.py:183
  17.3 7.9 %collective-permute-start.2 = (bf16[4,1,64,256]{3,2,1,0:T(8,128)(2,1)S(1)}, bf16[4,1,64,256]{3,2,1,0:T(8,128)(2,1)S(1)}, u32[]{:S(2)}, u32[]{:S(2)}) collective-permute-start(bf16[4,1,64,256]{3,2,1,0:T(8,128)(2,1)S(1)} %get-tuple-element.21), channel_id=1, source_target_pairs={{0,1},{1,2},{2,3},{3,0},{4,5},{5,6},{6,7},{7,4},{8,9},{9,10},{10,1... | collective-permute-start | bytes 393224 | tf_op jit(solution)/shard_map/ppermute | solution.py:182
  19.5 7.0 %collective-permute-start.3 = (bf16[4,1,64,256]{3,2,1,0:T(8,128)(2,1)S(1)}, bf16[4,1,64,256]{3,2,1,0:T(8,128)(2,1)S(1)}, u32[]{:S(2)}, u32[]{:S(2)}) collective-permute-start(bf16[4,1,64,256]{3,2,1,0:T(8,128)(2,1)S(1)} %get-tuple-element.20), channel_id=1, source_target_pairs={{1,0},{2,1},{3,2},{0,3},{5,4},{6,5},{7,6},{4,7},{9,8},{10,9},{11,1... | collective-permute-start | bytes 393224 | tf_op jit(solution)/shard_map/ppermute | solution.py:183
  26.6 34.3 %copy-start.14 = (bf16[256,169]{0,1:T(8,128)(2,1)S(1)}, bf16[256,169]{0,1:T(8,128)(2,1)}, u32[]{:S(2)}) copy-start(bf16[256,169]{0,1:T(8,128)(2,1)} %param.22) | copy-start | bytes 259588
  26.7 0.9 copy-start
  27.6 1.1 copy-start.2
  28.7 0.9 copy-start.5
  29.7 0.8 copy-start.8
  30.5 0.8 copy-start.10
  31.2 0.7 copy-start.12
  31.9 36.2 %copy-start.3 = (bf16[2,256,768]{2,1,0:T(8,128)(2,1)S(1)}, bf16[2,256,768]{2,1,0:T(8,128)(2,1)}, u32[]{:S(2)}) copy-start(bf16[2,256,768]{2,1,0:T(8,128)(2,1)} %w_qkv.3) | copy-start | bytes 2359300
  31.9 36.2 %copy-start.6 = (bf16[2,256,256]{2,1,0:T(8,128)(2,1)S(1)}, bf16[2,256,256]{2,1,0:T(8,128)(2,1)}, u32[]{:S(2)}) copy-start(bf16[2,256,256]{2,1,0:T(8,128)(2,1)} %w_edge.3) | copy-start | bytes 786436
  31.9 36.2 %copy-start.7 = (bf16[256,256]{1,0:T(8,128)(2,1)S(1)}, bf16[256,256]{1,0:T(8,128)(2,1)}, u32[]{:S(2)}) copy-start(bf16[256,256]{1,0:T(8,128)(2,1)} %rest_0_.1) | copy-start | bytes 393220
  31.9 36.2 %copy-start.9 = (s32[8192]{0:T(1024)S(1)}, s32[8192]{0:T(1024)}, u32[]{:S(2)}) copy-start(s32[8192]{0:T(1024)} %param.14) | copy-start | bytes 98308
  31.9 36.2 %copy-start.11 = (s32[8192]{0:T(1024)S(1)}, s32[8192]{0:T(1024)}, u32[]{:S(2)}) copy-start(s32[8192]{0:T(1024)} %param.15) | copy-start | bytes 98308
  31.9 36.2 %copy-start.13 = (f32[2,256]{1,0:T(2,128)S(1)}, f32[2,256]{1,0:T(2,128)}, u32[]{:S(2)}) copy-start(f32[2,256]{1,0:T(2,128)} %gains.3) | copy-start | bytes 6148
  52.1 2.0 copy-start.1
  55.2 4.4 %collective-permute-start.4 = (bf16[1,2,64,256]{3,2,1,0:T(8,128)(2,1)S(1)}, bf16[1,2,64,256]{3,2,1,0:T(8,128)(2,1)S(1)}, u32[]{:S(2)}, u32[]{:S(2)}) collective-permute-start(bf16[1,2,64,256]{3,2,1,0:T(8,128)(2,1)S(1)} %bitcast.117), channel_id=1, source_target_pairs={{0,4},{4,0},{1,5},{5,1},{2,6},{6,2},{3,7},{7,3},{8,12},{12,8},{9,1... | collective-permute-start | bytes 196616 | tf_op jit(solution)/shard_map/ppermute | solution.py:182
  56.0 4.3 %collective-permute-start.5 = (bf16[1,2,64,256]{3,2,1,0:T(8,128)(2,1)S(1)}, bf16[1,2,64,256]{3,2,1,0:T(8,128)(2,1)S(1)}, u32[]{:S(2)}, u32[]{:S(2)}) collective-permute-start(bf16[1,2,64,256]{3,2,1,0:T(8,128)(2,1)S(1)} %bitcast.115), channel_id=1, source_target_pairs={{4,0},{0,4},{5,1},{1,5},{6,2},{2,6},{7,3},{3,7},{12,8},{8,12},{13,... | collective-permute-start | bytes 196616 | tf_op jit(solution)/shard_map/ppermute | solution.py:183
  60.4 7.5 %collective-permute-start.6 = (bf16[4,1,64,256]{3,2,1,0:T(8,128)(2,1)S(1)}, bf16[4,1,64,256]{3,2,1,0:T(8,128)(2,1)S(1)}, u32[]{:S(2)}, u32[]{:S(2)}) collective-permute-start(bf16[4,1,64,256]{3,2,1,0:T(8,128)(2,1)S(1)} %get-tuple-element.19), channel_id=1, source_target_pairs={{0,1},{1,2},{2,3},{3,0},{4,5},{5,6},{6,7},{7,4},{8,9},{9,10},{10,1... | collective-permute-start | bytes 393224 | tf_op jit(solution)/shard_map/ppermute | solution.py:182
  61.1 6.9 %collective-permute-start.7 = (bf16[4,1,64,256]{3,2,1,0:T(8,128)(2,1)S(1)}, bf16[4,1,64,256]{3,2,1,0:T(8,128)(2,1)S(1)}, u32[]{:S(2)}, u32[]{:S(2)}) collective-permute-start(bf16[4,1,64,256]{3,2,1,0:T(8,128)(2,1)S(1)} %get-tuple-element.18), channel_id=1, source_target_pairs={{1,0},{2,1},{3,2},{0,3},{5,4},{6,5},{7,6},{4,7},{9,8},{10,9},{11,1... | collective-permute-start | bytes 393224 | tf_op jit(solution)/shard_map/ppermute | solution.py:183
  68.2 1.8 copy-start.4
Sparse Core Ops, SparseCore 0:
  101.4 128.6 all-reduce.2

commit v2 on v1

--- a/solution.py
+++ b/solution.py
@@ -172,22 +172,164 @@
     )(*operands)
 
 
-def with_halo(x, sides, width):
-    for axis, dim in sides:
-        count, length = (lax.axis_size(axis), x.shape[dim])
-        up = [(i, (i + 1) % count) for i in range(count)]
-        down = [(j, i) for i, j in up]
-        last = lax.slice_in_dim(x, length - width, length, axis=dim)
-        initial = lax.slice_in_dim(x, 0, width, axis=dim)
-        before = lax.ppermute(last, axis, up)
-        after = lax.ppermute(initial, axis, down)
-        x = jnp.concatenate([before, x, after], axis=dim)
-    return x
-
-
-def exchange(nodes, corner_index):
-    padded = with_halo(nodes[corner_index], (("gx", 0), ("gy", 1)), 1)
-    return jnp.concatenate([padded[i, j] for i, j in CELLS], axis=0)
+MESH = pl.DeviceIdType.MESH
+HALVES = ((-1, 1), (0, 0), (0, 1), (1, 0))
+
+
+def greet(devices):
+    barrier = pltpu.get_barrier_semaphore()
+    for device in devices:
+        pl.semaphore_signal(barrier, inc=1, device_id=device, device_id_type=MESH)
+    pl.semaphore_wait(barrier, len(devices))
+
+
+def halo_kernel(sizes, nodes, picks, out, cells, landed, send_sem, recv_sem):
+    rep, gx, gy = (lax.axis_index(a) for a in ("rep", "gx", "gy"))
+
+    def at(dx, dy):
+        return (rep, lax.rem(gx + sizes[0] + dx, sizes[0]), lax.rem(gy + sizes[1] + dy, sizes[1]))
+
+    offsets = [(i, j) for i in (-1, 0, 1) for j in (-1, 0, 1) if (i, j) != (0, 0)]
+    greet([at(i, j) for i, j in offsets])
+    atoms = nodes.shape[0]
+    rows = lax.broadcasted_iota(jnp.int32, (atoms, picks.shape[1]), 0)
+    picked_t = jnp.where(rows == picks[...], 1.0, 0.0).astype(F32)
+    cells[...] = nn(picked_t.T.astype(BF16), nodes[...]).astype(BF16).reshape(cells.shape)
+    copies = []
+    for c, (i, j) in enumerate(CELLS):
+        (dx, half_x), (dy, half_y) = HALVES[i], HALVES[j]
+        copy = pltpu.make_async_remote_copy(
+            src_ref=cells.at[half_x * 2 + half_y],
+            dst_ref=landed.at[c],
+            send_sem=send_sem.at[c],
+            recv_sem=recv_sem.at[c],
+            device_id=at(-dx, -dy),
+            device_id_type=MESH,
+        )
+        copy.start()
+        copies.append(copy)
+    for copy in copies:
+        copy.wait()
+    out[...] = landed[...].reshape(out.shape)
+
+
+def exchange(nodes, picks):
+    atoms, width = nodes.shape
+    cell_rows = picks.shape[1] // 4
+    vmem = pl.BlockSpec(memory_space=pltpu.VMEM)
+    sizes = (lax.axis_size("gx"), lax.axis_size("gy"))
+    return pl.pallas_call(
+        functools.partial(halo_kernel, sizes),
+        in_specs=[vmem, vmem],
+        out_specs=vmem,
+        out_shape=jax.ShapeDtypeStruct((len(CELLS) * cell_rows, width), BF16),
+        scratch_shapes=[
+            pltpu.VMEM((4, cell_rows, width), BF16),
+            pltpu.VMEM((len(CELLS), cell_rows, width), BF16),
+            pltpu.SemaphoreType.DMA((len(CELLS),)),
+            pltpu.SemaphoreType.DMA((len(CELLS),)),
+        ],
+        compiler_params=pltpu.CompilerParams(collective_id=0, has_side_effects=True),
+    )(nodes, picks)
+
+
+def sum_kernel(sizes, g_in, g_out, s_in, s_out, acc, total, *rest):
+    slots, (send_sem, recv_sem) = rest[:-2], rest[-2:]
+    rep, gx, gy = (lax.axis_index(a) for a in ("rep", "gx", "gy"))
+    n_rep, n_gx, n_gy = sizes
+    core, chip = lax.rem(rep, 2), lax.div(rep, 2)
+    groups = (
+        (2, core, lambda k: (chip * 2 + k, gx, gy)),
+        (n_rep // 2, chip, lambda k: (k * 2 + core, gx, gy)),
+        (n_gx, gx, lambda k: (rep, k, gy)),
+        (n_gy, gy, lambda k: (rep, gx, k)),
+    )
+    groups = [g for g in groups if g[0] > 1]
+    partners = [
+        [lax.rem(place + d, count) for d in range(1, count)] for count, place, _ in groups
+    ]
+    greet([group[2](k) for group, ks in zip(groups, partners) for k in ks])
+
+    parts, rows, lanes = acc.shape
+    quarter = parts // 4
+    cut = g_out.shape[1] - lanes
+    shape = (quarter, rows, lanes)
+    acc[:quarter] = g_in[:, :lanes].reshape(shape)
+    acc[quarter : 2 * quarter] = g_in[:, lanes:].reshape(shape)
+    acc[2 * quarter : 3 * quarter] = g_out[:, :lanes].reshape(shape)
+    acc[3 * quarter :] = jnp.pad(g_out[:, lanes:], ((0, 0), (0, lanes - cut))).reshape(shape)
+
+    used = 0
+
+    def send(src, dst, device):
+        nonlocal used
+        copy = pltpu.make_async_remote_copy(
+            src_ref=src,
+            dst_ref=dst,
+            send_sem=send_sem.at[used],
+            recv_sem=recv_sem.at[used],
+            device_id=device,
+            device_id_type=MESH,
+        )
+        used += 1
+        copy.start()
+        return copy
+
+    start, length, ranges = 0, parts, []
+    for (count, place, device), ks, slot in zip(groups, partners, slots):
+        length //= count
+        copies = [
+            send(acc.at[pl.ds(start + k * length, length)], slot.at[d], device(k))
+            for d, k in enumerate(ks)
+        ]
+        for copy in copies:
+            copy.wait()
+        start = start + place * length
+        mine = pl.ds(start, length)
+        value = acc[mine]
+        for d in range(count - 1):
+            value = value + slot[d]
+        acc[mine] = value
+        ranges.append(mine)
+    total[ranges[-1]] = acc[ranges[-1]]
+    for (count, place, device), ks, mine in reversed(list(zip(groups, partners, ranges))):
+        copies = [send(total.at[mine], total.at[mine], device(k)) for k in ks]
+        for copy in copies:
+            copy.wait()
+
+    flat = (quarter * rows, lanes)
+    s_in[:, :lanes] = total[:quarter].reshape(flat)
+    s_in[:, lanes:] = total[quarter : 2 * quarter].reshape(flat)
+    s_out[:, :lanes] = total[2 * quarter : 3 * quarter].reshape(flat)
+    s_out[:, lanes:] = total[3 * quarter :].reshape(flat)[:, :cut]
+
+
+def sum_all(grad_in, grad_out):
+    sizes = tuple(lax.axis_size(a) for a in ("rep", "gx", "gy"))
+    lanes = grad_in.shape[1] // 2
+    parts = sizes[0] * sizes[1] * sizes[2]
+    rows = 4 * grad_in.shape[0] // parts
+    counts = [c for c in (2, sizes[0] // 2, sizes[1], sizes[2]) if c > 1]
+    slots, length = [], parts
+    for count in counts:
+        length //= count
+        slots.append(pltpu.VMEM((count - 1, length, rows, lanes), F32))
+    copies = 2 * sum(c - 1 for c in counts)
+    vmem = pl.BlockSpec(memory_space=pltpu.VMEM)
+    return pl.pallas_call(
+        functools.partial(sum_kernel, sizes),
+        in_specs=[vmem, vmem],
+        out_specs=[vmem, vmem],
+        out_shape=[jax.ShapeDtypeStruct(g.shape, F32) for g in (grad_in, grad_out)],
+        scratch_shapes=[
+            pltpu.VMEM((parts, rows, lanes), F32),
+            pltpu.VMEM((parts, rows, lanes), F32),
+            *slots,
+            pltpu.SemaphoreType.DMA((copies,)),
+            pltpu.SemaphoreType.DMA((copies,)),
+        ],
+        compiler_params=pltpu.CompilerParams(collective_id=1, has_side_effects=True),
+    )(grad_in, grad_out)
 
 
 def body(
@@ -206,14 +348,14 @@
 ):
     slots = edge_feat.shape[0]
     layers = w_qkv.shape[0]
-    corner_index = send_idx.reshape(2, 2, send_idx.shape[-1])
+    picks = send_idx.reshape(1, 4 * send_idx.shape[-1])
     src = edge_src.reshape(1, slots)
     dst = edge_dst.reshape(1, slots)
     scale = 0.125 / (slots * lax.axis_size(("rep", "gx", "gy"))) ** 0.5
     nodes = node_feat
     edges = edge_feat
     for layer in range(layers):
-        ghosts = exchange(nodes, corner_index)
+        ghosts = exchange(nodes, picks)
         last = layer == layers - 1
         outs = run_layer(
             layer,
@@ -233,7 +375,7 @@
             nodes, grad_in, grad_out = outs
         else:
             nodes, edges = outs
-    grad_in, grad_out = lax.psum((grad_in, grad_out), ("rep", "gx", "gy"))
+    grad_in, grad_out = sum_all(grad_in, grad_out)
     return (nodes, grad_in, grad_out)
 
 

time: 241 us -> 130 us (0.54)
  waiting for transfers between devices: 144 us -> 0 us
  Pallas kernels: 51.4 us -> 108 us
  between operations: 15 us -> 1.49 us
  starting transfers between devices: 13.1 us -> 0 us
  local copies, waits for them, and re-layouts: 15.8 us -> 19.6 us
    psum x1 -> x0, waiting for transfers between devices: 129 us -> none  [body(): grad_in, grad_out = lax.psum((grad_in, grad_out), ('rep', 'gx', 'gy'))]
    pallas_call x0 -> x3, Pallas kernels: none -> 57.4 us  [the longest x1 30.9 us: sum_all(): pl.pallas_call(functools.partial(sum_kernel, sizes), in_specs=[vmem, vmem...]
    ppermute x8 -> x0, waiting for transfers between devices: 15.5 us -> none  [the longest x4 11.4 us: with_halo(): before = lax.ppermute(last, axis, up)]
    ppermute x8 -> x0, starting transfers between devices: 13.1 us -> none  [the longest x4 7.07 us: with_halo(): after = lax.ppermute(initial, axis, down)]
    unnamed x55 -> x43, local copies, waits for them, and re-layouts: 12.6 us -> 18.3 us
    gather x2 -> x0, local copies, waits for them, and re-layouts: 3.04 us -> none  [exchange(): padded = with_halo(nodes[corner_index], (('gx', 0), ('gy', 1)), 1)]
  transfers between devices with their start and end apart: 9 -> 0, of which waited for: 8 -> 0; matrix products, arithmetic and copies ran while one was open for 0% -> 0% of each run, Pallas kernels for 0% -> 0%
where the time goes in v2:
time: 130 us
  Pallas kernels  108 us (83%)
  local copies, waits for them, and re-layouts  19.6 us (15%)
  between operations  1.49 us (1%)
    pallas_call x2, Pallas kernels, run_layer(): pl.pallas_call(functools.partial(layer_kernel, layer, scale), grid=(slots...  51.1 us
    pallas_call x1, Pallas kernels, sum_all(): pl.pallas_call(functools.partial(sum_kernel, sizes), in_specs=[vmem, vmem...  30.9 us
    pallas_call x2, Pallas kernels, exchange(): pl.pallas_call(functools.partial(halo_kernel, sizes), in_specs=[vmem, vme...  26.5 us
    unnamed x43, local copies, waits for them, and re-layouts  18.3 us

profile of v2, /device:TPU:0, one launch (start us, length us, event | category | flops | bytes accessed | tf_op | source)
XLA Modules:
  0.0 129.6 jit_solution(14600326194266495060)
XLA Ops:
  0.6 0.0 copy-start.19
  0.6 0.0 copy-start.7
  0.7 0.0 copy-start.13
  0.7 0.0 copy-start.17
  0.7 0.0 copy-start.15
  1.4 1.3 %reshape.15.picks = s32[1,256]{1,0:T(1,128)} reshape(s32[1,1,1,2,2,64]{5,4,3,2,1,0:T(2,128)} %param.17) | data formatting | bytes 2048 | tf_op jit(solution)/shard_map/reshape | solution.py:351
  2.7 1.0 copy.15.rest_1_
  3.7 14.4 %shard_map.139.ghosts = bf16[768,256]{1,0:T(8,128)(2,1)} custom-call(bf16[256,256]{1,0:T(8,128)(2,1)} %nodes.3, s32[1,256]{1,0:T(1,128)} %reshape.15.picks), custom_call_target="tpu_custom_call" | custom-call | tf_op jit(solution)/shard_map/pallas_call | solution.py:221
  18.1 0.0 copy-start.1
  18.1 1.1 copy-done.1
  19.2 0.0 copy-start.5
  19.2 1.0 copy-done.5
  20.2 0.0 copy-start.6
  20.2 0.9 copy-done.6
  21.2 0.0 copy-start.10
  21.2 0.9 copy-done.10
  22.1 0.0 copy-start.14
  22.1 0.8 copy-done.14
  22.8 0.0 copy-start.16
  22.8 0.8 copy-done.16
  23.6 0.0 copy-start.18
  23.6 0.7 copy-done.18
  24.3 20.1 %shard_map.140 = (bf16[256,256]{1,0:T(8,128)(2,1)S(1)}, bf16[256,8192]{1,0:T(8,128)(2,1)S(1)}) custom-call(s32[1]{0:T(128)S(6)} %copy.18.count, bf16[256,256]{1,0:T(8,128)(2,1)S(1)} %copy-done.10, bf16[768,256]{1,0:T(8,128)(2,1)S(1)} %copy-done.5, bf16[2,256,768]{2,1,0:T(8,128)(2,1)S(1)} %copy-done.1, bf16[2,256,256]{2,1,0:T(8,128)(2,1)S(1)} %copy-done.6, ...), custom_call_target="tpu_custom_call" | custom-call | tf_op jit(solution)/shard_map/pallas_call | solution.py:162
  44.4 0.0 copy-start
  44.4 1.9 %copy-done = bf16[256,8192]{1,0:T(8,128)(2,1)} copy-done((bf16[256,8192]{1,0:T(8,128)(2,1)}, bf16[256,8192]{1,0:T(8,128)(2,1)S(1)}, u32[]{:S(2)}) %copy-start) | copy-done | bytes 4194328
  46.3 0.0 copy-start.8
  46.3 0.7 copy-done.8
  47.0 12.1 %shard_map.141.ghosts = bf16[768,256]{1,0:T(8,128)(2,1)} custom-call(bf16[256,256]{1,0:T(8,128)(2,1)} %copy-done.8, s32[1,256]{1,0:T(1,128)} %reshape.15.picks), custom_call_target="tpu_custom_call" | custom-call | tf_op jit(solution)/shard_map/pallas_call | solution.py:221
  59.1 0.0 copy-done.19
  59.1 0.0 copy-done.7
  59.1 0.0 copy-done.13
  59.1 0.0 copy-done.17
  59.1 0.0 copy-done.15
  59.1 0.0 copy-done.2
  59.1 0.0 copy-start.3
  59.2 1.8 %copy-done.3 = bf16[169,8192]{1,0:T(8,128)(2,1)S(1)} copy-done((bf16[169,8192]{1,0:T(8,128)(2,1)S(1)}, bf16[169,8192]{1,0:T(8,128)(2,1)}, u32[]{:S(2)}) %copy-start.3) | copy-done | bytes 2768920
  61.0 0.0 copy-start.4
  61.0 1.0 copy-done.4
  62.0 0.0 copy-start.9
  62.0 0.9 copy-done.9
  62.9 31.0 %shard_map.142 = (bf16[256,256]{1,0:T(8,128)(2,1)}, f32[256,256]{1,0:T(8,128)S(1)}, f32[256,169]{1,0:T(8,128)S(1)}) custom-call(s32[1]{0:T(128)S(6)} %copy.18.count, bf16[256,256]{1,0:T(8,128)(2,1)S(1)} %copy-done.9, bf16[768,256]{1,0:T(8,128)(2,1)S(1)} %copy-done.4, bf16[2,256,768]{2,1,0:T(8,128)(2,1)S(1)} %copy-done.2, bf16[2,256,256]{2,1,0:T(8,128)(2,1)S(1)} %copy-done.7, ...), custom_call_target="tpu_custom_call" | custom-call | tf_op jit(solution)/shard_map/pallas_call | solution.py:162
  93.9 0.0 copy-start.11
  93.9 0.7 copy-done.11
  94.6 0.0 copy-start.12
  94.6 0.7 copy-done.12
  95.3 30.9 %shard_map.143 = (f32[256,256]{1,0:T(8,128)}, f32[256,169]{1,0:T(8,128)}) custom-call(f32[256,256]{1,0:T(8,128)} %copy-done.11, f32[256,169]{1,0:T(8,128)} %copy-done.12), custom_call_target="tpu_custom_call" | custom-call | tf_op jit(solution)/shard_map/pallas_call | solution.py:319
  126.2 1.7 %copy.16 = f32[256,169]{0,1:T(8,128)} copy(f32[256,169]{1,0:T(8,128)} %get-tuple-element.19) | data formatting | bytes 346112
  127.9 1.7 %copy.19 = f32[256,256]{1,0:T(8,128)} copy(f32[256,256]{1,0:T(8,128)} %get-tuple-element.24) | data formatting | bytes 524288
  (1 shorter events, 0.0 us)
Async XLA Ops:
  0.6 58.5 %copy-start.19 = (f32[2,256]{1,0:T(2,128)S(1)}, f32[2,256]{1,0:T(2,128)}, u32[]{:S(2)}) copy-start(f32[2,256]{1,0:T(2,128)} %gains.3) | copy-start | bytes 6148
  0.6 58.4 %copy-start.7 = (bf16[2,256,256]{2,1,0:T(8,128)(2,1)S(1)}, bf16[2,256,256]{2,1,0:T(8,128)(2,1)}, u32[]{:S(2)}) copy-start(bf16[2,256,256]{2,1,0:T(8,128)(2,1)} %w_edge.3) | copy-start | bytes 786436
  0.7 58.4 %copy-start.13 = (bf16[256,256]{1,0:T(8,128)(2,1)S(1)}, bf16[256,256]{1,0:T(8,128)(2,1)}, u32[]{:S(2)}) copy-start(bf16[256,256]{1,0:T(8,128)(2,1)} %rest_0_.1) | copy-start | bytes 393220
  0.7 58.4 %copy-start.17 = (s32[8192]{0:T(1024)S(1)}, s32[8192]{0:T(1024)}, u32[]{:S(2)}) copy-start(s32[8192]{0:T(1024)} %param.15) | copy-start | bytes 98308
  0.7 58.4 %copy-start.15 = (s32[8192]{0:T(1024)S(1)}, s32[8192]{0:T(1024)}, u32[]{:S(2)}) copy-start(s32[8192]{0:T(1024)} %param.14) | copy-start | bytes 98308
  18.1 1.1 copy-start.1
  19.2 1.0 copy-start.5
  20.2 0.9 copy-start.6
  21.2 0.9 copy-start.10
  22.1 0.8 copy-start.14
  22.8 0.8 copy-start.16
  23.6 0.7 copy-start.18
  24.3 34.9 %copy-start.2 = (bf16[2,256,768]{2,1,0:T(8,128)(2,1)S(1)}, bf16[2,256,768]{2,1,0:T(8,128)(2,1)}, u32[]{:S(2)}) copy-start(bf16[2,256,768]{2,1,0:T(8,128)(2,1)} %w_qkv.3) | copy-start | bytes 2359300
  44.4 1.9 %copy-start = (bf16[256,8192]{1,0:T(8,128)(2,1)}, bf16[256,8192]{1,0:T(8,128)(2,1)S(1)}, u32[]{:S(2)}) copy-start(bf16[256,8192]{1,0:T(8,128)(2,1)S(1)} %get-tuple-element.11.edges) | copy-start | bytes 12582916
  46.3 0.7 copy-start.8
  59.1 1.8 %copy-start.3 = (bf16[169,8192]{1,0:T(8,128)(2,1)S(1)}, bf16[169,8192]{1,0:T(8,128)(2,1)}, u32[]{:S(2)}) copy-start(bf16[169,8192]{1,0:T(8,128)(2,1)} %rest_2_.1) | copy-start | bytes 8306692
  61.0 1.0 copy-start.4
  62.0 0.9 copy-start.9
  93.9 0.7 copy-start.11
  94.6 0.7 copy-start.12

commit v3 on v1

v3 whole, which is shorter than its diff:
```python
import functools

import jax
import jax.numpy as jnp
from jax import lax
from jax.experimental import pallas as pl
from jax.experimental.pallas import tpu as pltpu
from jax.sharding import PartitionSpec as P

F32 = jnp.float32
BF16 = jnp.bfloat16
BLOCK = 1024
SUB = 512
CELLS = tuple((i, j) for i in range(4) for j in range(4) if not (i in (1, 2) and j in (1, 2)))
NT = (((1,), (1,)), ((), ()))


def nn(a, b):
    return jnp.dot(a, b, preferred_element_type=F32)


def nt(a, b):
    return lax.dot_general(a, b, NT, preferred_element_type=F32)


def sigmoid(v):
    return 0.5 * jnp.tanh(0.5 * v) + 0.5


def hot(rows_iota, row, base):
    picked = jnp.where((row >= base) & (row < base + 256), row - base, -1)
    picked = picked.astype(F32).astype(BF16)
    return jnp.where(rows_iota == picked, jnp.ones((), BF16), jnp.zeros((), BF16))


def edge_step(edges_t, src, dst, live, iota, kv_t, q_t, we_t):
    dst_hot = hot(iota, dst, 0)
    table_rows = kv_t.shape[1]
    gathered = nn(kv_t[:, :256], hot(iota, src, 0))
    for base in range(256, table_rows, 256):
        gathered = gathered + nn(kv_t[:, base : base + 256], hot(iota, src, base))
    pre = gathered[:256] + nn(q_t[...], dst_hot) + nn(we_t[...], edges_t)
    gate = live * sigmoid(pre)
    new_edges = (edges_t.astype(F32) + gate * pre).astype(BF16)
    weighted = gate * gathered[256:]
    high = weighted.astype(BF16)
    low = (weighted - high.astype(F32)).astype(BF16)
    added = nt(jnp.concatenate([high, low], axis=0), dst_hot)
    return new_edges, added[:256] + added[256:]


def update_nodes(nodes, summed_t, gain):
    summed = summed_t.T
    centre = summed - jnp.mean(summed, axis=-1, keepdims=True)
    spread = jnp.mean(centre * centre, axis=-1, keepdims=True)
    return (nodes.astype(F32) + gain * (centre * lax.rsqrt(spread + 1e-05))).astype(BF16)


MESH = pl.DeviceIdType.MESH
HALVES = ((-1, 1), (0, 0), (0, 1), (1, 0))


def greet(devices):
    barrier = pltpu.get_barrier_semaphore()
    for device in devices:
        pl.semaphore_signal(barrier, inc=1, device_id=device, device_id_type=MESH)
    pl.semaphore_wait(barrier, len(devices))


def whole_kernel(
    sizes,
    layers,
    scale,
    count,
    nodes_in,
    picks,
    w_qkv,
    w_edge,
    gains,
    head_in,
    head_out,
    edges_in,
    src,
    dst,
    targets,
    out_nodes,
    s_in,
    s_out,
    nodes,
    edges,
    kv_t,
    q_t,
    we_t,
    iota,
    summed,
    head_in_t,
    head_out_t,
    g_in,
    g_out,
    cells,
    landed,
    acc,
    total,
    *rest,
):
    slots, (halo_send, halo_recv, sum_send, sum_recv) = rest[:-4], rest[-4:]
    step = pl.program_id(0)
    blocks = edges.shape[0]
    rep, gx, gy = (lax.axis_index(name) for name in ("rep", "gx", "gy"))
    n_rep, n_gx, n_gy = sizes

    def at(dx, dy):
        return (rep, lax.rem(gx + n_gx + dx, n_gx), lax.rem(gy + n_gy + dy, n_gy))

    core, chip = lax.rem(rep, 2), lax.div(rep, 2)
    groups = (
        (2, core, lambda k: (chip * 2 + k, gx, gy)),
        (
            (n_rep // 2) * n_gx,
            chip * n_gx + gx,
            lambda k: (lax.div(k, n_gx) * 2 + core, lax.rem(k, n_gx), gy),
        ),
        (n_gy, gy, lambda k: (rep, gx, k)),
    )
    partners = [
        [lax.rem(place + d, size) for d in range(1, size)] for size, place, _ in groups
    ]

    def send(src_ref, dst_ref, send_sem, recv_sem, device):
        copy = pltpu.make_async_remote_copy(
            src_ref=src_ref,
            dst_ref=dst_ref,
            send_sem=send_sem,
            recv_sem=recv_sem,
            device_id=device,
            device_id_type=MESH,
        )
        copy.start()
        return copy

    def exchange(layer):
        atoms = nodes.shape[0]
        rows = lax.broadcasted_iota(jnp.int32, (atoms, picks.shape[1]), 0)
        picked_t = jnp.where(rows == picks[...], 1.0, 0.0).astype(F32)
        cells[...] = nn(picked_t.T.astype(BF16), nodes[...]).astype(BF16).reshape(cells.shape)
        copies = []
        for c, (i, j) in enumerate(CELLS):
            (dx, half_x), (dy, half_y) = HALVES[i], HALVES[j]
            copies.append(
                send(
                    cells.at[half_x * 2 + half_y],
                    landed.at[layer, c],
                    halo_send.at[layer, c],
                    halo_recv.at[layer, c],
                    at(-dx, -dy),
                )
            )
        w_t = w_qkv[0].T
        q_t[...] = nt(w_t[:256], nodes[...]).astype(BF16)
        kv_t[:, :atoms] = nt(w_t[256:], nodes[...]).astype(BF16)
        we_t[...] = w_edge[0].T
        summed[...] = jnp.zeros_like(summed)
        for copy in copies:
            copy.wait()
        ghosts = landed[layer].reshape(len(CELLS) * cells.shape[1], cells.shape[2])
        kv_t[:, atoms:] = nt(w_t[256:], ghosts).astype(BF16)

    def sum_all():
        parts, rows, lanes = acc.shape
        quarter = parts // 4
        cut = g_out.shape[1] - lanes
        shape = (quarter, rows, lanes)
        acc[:quarter] = g_in[:, :lanes].reshape(shape)
        acc[quarter : 2 * quarter] = g_in[:, lanes:].reshape(shape)
        acc[2 * quarter : 3 * quarter] = g_out[:, :lanes].reshape(shape)
        acc[3 * quarter :] = jnp.pad(g_out[:, lanes:], ((0, 0), (0, lanes - cut))).reshape(shape)
        used, start, length, ranges = 0, 0, parts, []
        for (size, place, device), ks, slot in zip(groups, partners, slots):
            length //= size
            copies = []
            for d, k in enumerate(ks):
                piece = acc.at[pl.ds(start + k * length, length)]
                copies.append(
                    send(piece, slot.at[d], sum_send.at[used], sum_recv.at[used], device(k))
                )
                used += 1
            for copy in copies:
                copy.wait()
            start = start + place * length
            mine = pl.ds(start, length)
            value = acc[mine]
            for d in range(size - 1):
                value = value + slot[d]
            acc[mine] = value
            ranges.append(mine)
        total[ranges[-1]] = acc[ranges[-1]]
        for (size, place, device), ks, mine in reversed(list(zip(groups, partners, ranges))):
            copies = []
            for k in ks:
                piece = total.at[mine]
                copies.append(
                    send(piece, piece, sum_send.at[used], sum_recv.at[used], device(k))
                )
                used += 1
            for copy in copies:
                copy.wait()
        flat = (quarter * rows, lanes)
        s_in[:, :lanes] = total[:quarter].reshape(flat)
        s_in[:, lanes:] = total[quarter : 2 * quarter].reshape(flat)
        s_out[:, :lanes] = total[2 * quarter : 3 * quarter].reshape(flat)
        s_out[:, lanes:] = total[3 * quarter :].reshape(flat)[:, :cut]

    def edge_block(layer, block):
        for part in range(BLOCK // SUB):
            lanes = slice(part * SUB, (part + 1) * SUB)
            position = block * BLOCK + part * SUB + lax.broadcasted_iota(jnp.int32, (1, SUB), 1)
            live = jnp.where(position < count[0], 1.0, 0.0).astype(F32)
            edges_t = edges_in[lanes, :].T if layer == 0 else edges[block, :, lanes]
            new_edges, added = edge_step(
                edges_t, src[:, lanes], dst[:, lanes], live, iota[...], kv_t, q_t, we_t
            )
            summed[...] += added
            if layer < layers - 1:
                edges[block, :, lanes] = new_edges
                continue
            act = nn(head_in_t[...], new_edges)
            sig = sigmoid(act)
            hidden = (act * sig).astype(BF16)
            pred = nn(head_out_t[...], hidden)
            dpred = (live * (pred - targets[:, lanes].astype(F32)) * scale).astype(BF16)
            dhidden = nn(head_out[...], dpred)
            dact = (dhidden * sig * (1.0 + act * (1.0 - sig))).astype(BF16)
            g_in[...] += nt(new_edges, dact)
            g_out[...] += nt(hidden, dpred)

    @pl.when(step == 0)
    def _():
        offsets = [(i, j) for i in (-1, 0, 1) for j in (-1, 0, 1) if (i, j) != (0, 0)]
        greet(
            [at(i, j) for i, j in offsets]
            + [group[2](k) for group, ks in zip(groups, partners) for k in ks]
        )
        nodes[...] = nodes_in[...]
        iota[...] = lax.broadcasted_iota(jnp.int32, iota.shape, 0).astype(F32).astype(BF16)
        head_in_t[...] = head_in[...].T
        head_out_t[...] = head_out[...].T
        g_in[...] = jnp.zeros_like(g_in)
        g_out[...] = jnp.zeros_like(g_out)

    for layer in range(layers):
        first = layer * blocks

        @pl.when(step == first)
        def _():
            exchange(layer)

        @pl.when((step >= first) & (step < first + blocks))
        def _():
            edge_block(layer, step - first)

        @pl.when(step == first + blocks - 1)
        def _():
            nodes[...] = update_nodes(nodes[...], summed[...], gains[layer : layer + 1, :])

    @pl.when(step == layers * blocks - 1)
    def _():
        out_nodes[...] = nodes[...]
        sum_all()


def body(
    node_feat,
    edge_feat,
    edge_src,
    edge_dst,
    edge_count,
    send_idx,
    w_qkv,
    w_edge,
    gains,
    head_in,
    head_out,
    targets,
):
    slots, width = edge_feat.shape
    atoms = node_feat.shape[0]
    layers = w_qkv.shape[0]
    cell_rows = send_idx.shape[-1]
    sizes = tuple(lax.axis_size(name) for name in ("rep", "gx", "gy"))
    devices = sizes[0] * sizes[1] * sizes[2]
    scale = 0.125 / (slots * devices) ** 0.5
    blocks = slots // BLOCK
    lanes = width // 2
    rows = 4 * width // devices
    sum_slots, length, copies = [], devices, 0
    for size in (2, sizes[0] // 2 * sizes[1], sizes[2]):
        length //= size
        copies += 2 * (size - 1)
        sum_slots.append(pltpu.VMEM((size - 1, length, rows, lanes), F32))
    whole = lambda a: pl.BlockSpec(a.shape, lambda i: (0,) * a.ndim)
    by_layer = lambda a: pl.BlockSpec((1,) + a.shape[1:], lambda i: (lax.div(i, blocks), 0, 0))
    row = pl.BlockSpec((1, BLOCK), lambda i: (0, lax.rem(i, blocks)))
    skipped = (layers - 1) * blocks
    picks = send_idx.reshape(1, 4 * cell_rows)
    orb = head_out.shape[1]
    return pl.pallas_call(
        functools.partial(whole_kernel, sizes, layers, scale),
        grid=(layers * blocks,),
        in_specs=[
            pl.BlockSpec(memory_space=pltpu.SMEM),
            whole(node_feat),
            whole(picks),
            by_layer(w_qkv),
            by_layer(w_edge),
            whole(gains),
            whole(head_in),
            whole(head_out),
            pl.BlockSpec((BLOCK, width), lambda i: (jnp.minimum(i, blocks - 1), 0)),
            row,
            row,
            pl.BlockSpec((orb, BLOCK), lambda i: (0, jnp.maximum(i - skipped, 0))),
        ],
        out_specs=[whole(node_feat), whole(head_in), whole(head_out)],
        out_shape=[
            jax.ShapeDtypeStruct(node_feat.shape, BF16),
            jax.ShapeDtypeStruct(head_in.shape, F32),
            jax.ShapeDtypeStruct(head_out.shape, F32),
        ],
        scratch_shapes=[
            pltpu.VMEM((atoms, width), BF16),
            pltpu.VMEM((blocks, width, BLOCK), BF16),
            pltpu.VMEM((2 * width, atoms + len(CELLS) * cell_rows), BF16),
            pltpu.VMEM((width, atoms), BF16),
            pltpu.VMEM((width, width), BF16),
            pltpu.VMEM((256, SUB), BF16),
            pltpu.VMEM((width, atoms), F32),
            pltpu.VMEM(head_in.shape[::-1], BF16),
            pltpu.VMEM(head_out.shape[::-1], BF16),
            pltpu.VMEM(head_in.shape, F32),
            pltpu.VMEM(head_out.shape, F32),
            pltpu.VMEM((4, cell_rows, width), BF16),
            pltpu.VMEM((layers, len(CELLS), cell_rows, width), BF16),
            pltpu.VMEM((devices, rows, lanes), F32),
            pltpu.VMEM((devices, rows, lanes), F32),
            *sum_slots,
            pltpu.SemaphoreType.DMA((layers, len(CELLS))),
            pltpu.SemaphoreType.DMA((layers, len(CELLS))),
            pltpu.SemaphoreType.DMA((copies,)),
            pltpu.SemaphoreType.DMA((copies,)),
        ],
        compiler_params=pltpu.CompilerParams(
            dimension_semantics=("arbitrary",),
            collective_id=0,
            has_side_effects=True,
            vmem_limit_bytes=48 << 20,
        ),
    )(
        edge_count,
        node_feat,
        picks,
        w_qkv,
        w_edge,
        gains,
        head_in,
        head_out,
        edge_feat,
        edge_src.reshape(1, slots),
        edge_dst.reshape(1, slots),
        targets,
    )


def solution(mesh):
    tiles = ("rep", "gx", "gy")
    return jax.shard_map(
        body,
        mesh=mesh,
        in_specs=(
            P(tiles, None),
            P(tiles, None),
            P(tiles),
            P(tiles),
            P(tiles),
            P("rep", "gx", "gy", None, None, None),
            P(),
            P(),
            P(),
            P(),
            P(),
            P(None, tiles),
        ),
        out_specs=(P(tiles, None), P(), P()),
        check_vma=False,
    )
```

time: 241 us -> 107 us (0.44)
  waiting for transfers between devices: 144 us -> 0 us
  Pallas kernels: 51.4 us -> 93 us
  between operations: 15 us -> 1.31 us
  starting transfers between devices: 13.1 us -> 0 us
  local copies, waits for them, and re-layouts: 15.8 us -> 11.8 us
    psum x1 -> x0, waiting for transfers between devices: 129 us -> none  [body(): grad_in, grad_out = lax.psum((grad_in, grad_out), ('rep', 'gx', 'gy'))]
    pallas_call x2 -> x1, Pallas kernels: 51.4 us -> 93 us  [body(): pl.pallas_call(functools.partial(whole_kernel, sizes, layers, scale), gri...]
    ppermute x8 -> x0, waiting for transfers between devices: 15.5 us -> none  [the longest x4 11.4 us: with_halo(): before = lax.ppermute(last, axis, up)]
    ppermute x8 -> x0, starting transfers between devices: 13.1 us -> none  [the longest x4 7.07 us: with_halo(): after = lax.ppermute(initial, axis, down)]
    gather x2 -> x0, local copies, waits for them, and re-layouts: 3.04 us -> none  [exchange(): padded = with_halo(nodes[corner_index], (('gx', 0), ('gy', 1)), 1)]
    unnamed x55 -> x19, local copies, waits for them, and re-layouts: 12.6 us -> 10.2 us
  transfers between devices with their start and end apart: 9 -> 0, of which waited for: 8 -> 0; matrix products, arithmetic and copies ran while one was open for 0% -> 0% of each run, Pallas kernels for 0% -> 0%
where the time goes in v3:
time: 107 us; the launch traced here: 106 us
  Pallas kernels  93 us (87%)
  local copies, waits for them, and re-layouts  11.8 us (11%)
  between operations  1.31 us (1%)
    pallas_call x1, Pallas kernels, body(): pl.pallas_call(functools.partial(whole_kernel, sizes, layers, scale), gri...  93 us
    unnamed x19, local copies, waits for them, and re-layouts  10.2 us

profile of v3, /device:TPU:0, one launch (start us, length us, event | category | flops | bytes accessed | tf_op | source)
XLA Modules:
  0.0 106.1 jit_solution(7162045868510468909)
XLA Ops:
  1.3 0.8 reshape.15.picks
  2.0 1.0 copy.15.head_out
  3.0 0.0 copy-start
  3.0 1.8 %copy-done = bf16[169,8192]{1,0:T(8,128)(2,1)S(1)} copy-done((bf16[169,8192]{1,0:T(8,128)(2,1)S(1)}, bf16[169,8192]{1,0:T(8,128)(2,1)}, u32[]{:S(2)}) %copy-start) | copy-done | bytes 2768920
  4.9 0.0 copy-start.1
  4.9 1.1 %copy-done.1 = bf16[2,256,768]{2,1,0:T(8,128)(2,1)S(1)} copy-done((bf16[2,256,768]{2,1,0:T(8,128)(2,1)S(1)}, bf16[2,256,768]{2,1,0:T(8,128)(2,1)}, u32[]{:S(2)}) %copy-start.1) | copy-done | bytes 786456
  6.0 0.0 copy-start.2
  6.0 0.9 copy-done.2
  6.9 0.0 copy-start.3
  6.9 0.9 copy-done.3
  7.8 0.0 copy-start.4
  7.8 0.9 copy-done.4
  8.7 0.0 copy-start.5
  8.7 0.8 copy-done.5
  9.5 0.0 copy-start.6
  9.5 0.8 copy-done.6
  10.3 0.0 copy-start.7
  10.3 0.7 copy-done.7
  10.9 93.0 %shard_map.139 = (bf16[256,256]{1,0:T(8,128)(2,1)S(1)}, f32[256,256]{1,0:T(8,128)S(1)}, f32[256,169]{1,0:T(8,128)S(1)}) custom-call(s32[1]{0:T(128)S(6)} %copy.19.count, bf16[256,256]{1,0:T(8,128)(2,1)S(1)} %copy-done.3, s32[1,256]{1,0:T(1,128)S(1)} %reshape.15.picks, bf16[2,256,768]{2,1,0:T(8,128)(2,1)S(1)} %copy-done.1, ...), custom_call_target="tpu_custom_call" | custom-call | tf_op jit(solution)/shard_map/pallas_call | solution.py:306
  103.9 0.8 copy.16
  104.7 0.7 copy.20
  105.4 0.7 copy.21
Async XLA Ops:
  3.0 1.8 %copy-start = (bf16[169,8192]{1,0:T(8,128)(2,1)S(1)}, bf16[169,8192]{1,0:T(8,128)(2,1)}, u32[]{:S(2)}) copy-start(bf16[169,8192]{1,0:T(8,128)(2,1)} %targets.1) | copy-start | bytes 8306692
  4.9 1.1 %copy-start.1 = (bf16[2,256,768]{2,1,0:T(8,128)(2,1)S(1)}, bf16[2,256,768]{2,1,0:T(8,128)(2,1)}, u32[]{:S(2)}) copy-start(bf16[2,256,768]{2,1,0:T(8,128)(2,1)} %w_qkv.1) | copy-start | bytes 2359300
  6.0 0.9 copy-start.2
  6.9 0.9 copy-start.3
  7.8 0.9 copy-start.4
  8.7 0.8 copy-start.5
  9.5 0.8 copy-start.6
  10.3 0.7 copy-start.7

commit v4 on v3

--- a/solution.py
+++ b/solution.py
@@ -352,7 +352,7 @@
             dimension_semantics=("arbitrary",),
             collective_id=0,
             has_side_effects=True,
-            vmem_limit_bytes=48 << 20,
+            vmem_limit_bytes=60 << 20,
         ),
     )(
         edge_count,

time: 107 us -> 104 us (0.972); the launches traced: 106 us -> 104 us
  local copies, waits for them, and re-layouts: 11.8 us -> 7.94 us
  Pallas kernels: 93 us -> 95 us
    unnamed x19 -> x3, local copies, waits for them, and re-layouts: 10.2 us -> 4.88 us
    pallas_call x1, Pallas kernels: 93 us -> 95 us  [body(): pl.pallas_call(functools.partial(whole_kernel, sizes, layers, scale), gri...]
where the time goes in v4:
time: 104 us
  Pallas kernels  95 us (91%)
  local copies, waits for them, and re-layouts  7.94 us (8%)
  between operations  1.29 us (1%)
    pallas_call x1, Pallas kernels, body(): pl.pallas_call(functools.partial(whole_kernel, sizes, layers, scale), gri...  95 us
    unnamed x3, local copies, waits for them, and re-layouts  4.88 us

profile of v4, /device:TPU:0, one launch (start us, length us, event | category | flops | bytes accessed | tf_op | source)
XLA Modules:
  0.0 104.2 jit_solution(3366456920016250628)
XLA Ops:
  1.3 1.3 %reshape.15.picks = s32[1,256]{1,0:T(1,128)} reshape(s32[1,1,1,2,2,64]{5,4,3,2,1,0:T(2,128)} %param.17) | data formatting | bytes 2048 | tf_op jit(solution)/shard_map/reshape | solution.py:304
  2.6 1.6 %copy.15.head_out = bf16[256,169]{1,0:T(8,128)(2,1)} copy(bf16[256,169]{0,1:T(8,128)(2,1)} %param.22) | data formatting | bytes 173056 | tf_op args[10]
  4.2 95.0 %shard_map.139 = (bf16[256,256]{1,0:T(8,128)(2,1)}, f32[256,256]{1,0:T(8,128)}, f32[256,169]{1,0:T(8,128)}) custom-call(s32[1]{0:T(128)S(6)} %copy.19.count, bf16[256,256]{1,0:T(8,128)(2,1)} %nodes_in.1, s32[1,256]{1,0:T(1,128)} %reshape.15.picks, bf16[2,256,768]{2,1,0:T(8,128)(2,1)} %w_qkv.1, bf16[2,256,256]{2,1,0:T(8,128)(2,1)} %w_edge.1, f32[2,256]{1,0:T(2,128)} %gains.1, ...), custom_call_target="tpu_custom_call" | custom-call | tf_op jit(solution)/shard_map/pallas_call | solution.py:306
  99.2 1.7 %copy.16 = f32[256,169]{0,1:T(8,128)} copy(f32[256,169]{1,0:T(8,128)} %get-tuple-element.5) | data formatting | bytes 346112 | tf_op jit(solution)/shard_map/pallas_call | solution.py:306
  101.0 1.6 %copy.20 = bf16[256,256]{1,0:T(8,128)(2,1)} copy(bf16[256,256]{1,0:T(8,128)(2,1)} %get-tuple-element.9) | data formatting | bytes 262144
  102.5 1.7 %copy.21 = f32[256,256]{1,0:T(8,128)} copy(f32[256,256]{1,0:T(8,128)} %get-tuple-element.10) | data formatting | bytes 524288
